TPU v7x, 256 devices: a whole 4x4x8 slice. The times are simulated.
256 devices in a mesh: row: 8 (over y_lo, x), col: 32 (over z, y_hi, core).
Axes of the slice: x: 4, y: 4 (y_hi: 2, y_lo: 2; y = y_hi * 2 + y_lo), z: 8, core: 2. Of those that a mesh axis runs over, the one named last changes fastest.
Arguments:
- pair: bfloat16 [512, 512, 128], P('row', 'col'), may hold values from -6 to 6
- residue_mask: int32 [512], replicated, may hold values 0 or 1
- in_gain: float32 [2, 128], replicated, may hold values from 0.25 to 1.75
- in_bias: float32 [2, 128], replicated, may hold values from -3 to 3
- proj_weight: bfloat16 [2, 128, 512], replicated, may hold values from -0.5 to 0.5
- gate_weight: bfloat16 [2, 128, 128], replicated, may hold values from -0.5 to 0.5
- out_gain: float32 [2, 128], replicated, may hold values from 0.25 to 1.75
- out_bias: float32 [2, 128], replicated, may hold values from -3 to 3
- out_weight: bfloat16 [2, 128, 128], replicated, may hold values from -0.5 to 0.5
Outputs:
- updated: bfloat16 [512, 512, 128], P('row', 'col')
All inputs are finite; a program needn't handle non-finite values.
Results may differ from a plain program's by a relative error of at most 0.012.
Values may be sent and summed in bfloat16 or wider, within the bound.
A program may use at most 128 MiB of HBM per device.

v0:
```python
import jax
import jax.numpy as jnp
from jax import lax
from jax.sharding import PartitionSpec as P


def layer_norm(values, gain, bias):
    center = values - jnp.mean(values, axis=-1, keepdims=True)
    spread = jnp.mean(center * center, axis=-1, keepdims=True)
    return center * lax.rsqrt(spread + 1e-05) * gain + bias


def factors(tile, mask_rows, mask_cols, gain, bias, w_proj, w_gate):
    rows_here, cols_here, width = tile.shape
    hidden = w_proj.shape[1] // 4
    normed = layer_norm(tile.astype(jnp.float32), gain, bias).astype(jnp.bfloat16)
    flat = normed.reshape(rows_here * cols_here, width)
    proj = jnp.dot(flat, w_proj, preferred_element_type=jnp.float32).reshape(
        rows_here, cols_here, 4 * hidden
    )
    masking = (mask_rows[:, None] * mask_cols[None, :])[:, :, None]
    left = (jax.nn.sigmoid(proj[..., :hidden]) * proj[..., hidden : 2 * hidden] * masking).astype(
        jnp.bfloat16
    )
    right = (
        jax.nn.sigmoid(proj[..., 2 * hidden : 3 * hidden]) * proj[..., 3 * hidden :] * masking
    ).astype(jnp.bfloat16)
    gated = jax.nn.sigmoid(jnp.dot(flat, w_gate, preferred_element_type=jnp.float32)).reshape(
        rows_here, cols_here, width
    )
    return (left, right, gated)


def collect_rows(tile):
    return lax.all_gather(tile, "row", axis=0, tiled=True)


def regroup_cols(tile):
    gathered = collect_rows(tile)
    return lax.all_to_all(gathered, "col", split_axis=0, concat_axis=1, tiled=True)


def panel_product(left, right):
    return jnp.einsum(
        "ikc,jkc->ijc",
        lax.all_gather(left, "col", axis=1, tiled=True),
        right,
        preferred_element_type=jnp.float32,
    )


def shards(
    pair, residue_mask, in_gain, in_bias, proj_weight, gate_weight, out_gain, out_bias, out_weight
):
    tile_rows, tile_cols, width = pair.shape
    row_index = lax.axis_index("row")
    col_index = lax.axis_index("col")
    mask = residue_mask.astype(jnp.float32)
    mask_rows = lax.dynamic_slice_in_dim(mask, row_index * tile_rows, tile_rows, 0)
    mask_cols = lax.dynamic_slice_in_dim(mask, col_index * tile_cols, tile_cols, 0)
    current = pair
    for layer in range(2):
        incoming = layer == 1
        left, right, gated = factors(
            current,
            mask_rows,
            mask_cols,
            in_gain[layer],
            in_bias[layer],
            proj_weight[layer],
            gate_weight[layer],
        )
        if incoming:
            spread_left = regroup_cols(left)
            own_cols = lax.dynamic_slice_in_dim(spread_left, row_index * tile_rows, tile_rows, 1)
            left_tile = jnp.transpose(own_cols, (1, 0, 2))
            right_rows = jnp.transpose(collect_rows(right), (1, 0, 2))
            mixed = panel_product(left_tile, right_rows)
        else:
            mixed = panel_product(left, regroup_cols(right))
        normed = layer_norm(mixed, out_gain[layer], out_bias[layer]).astype(jnp.bfloat16)
        hidden = normed.shape[2]
        update = jnp.dot(
            normed.reshape(tile_rows * tile_cols, hidden),
            out_weight[layer],
            preferred_element_type=jnp.float32,
        ).reshape(tile_rows, tile_cols, width)
        current = (current.astype(jnp.float32) + gated * update).astype(jnp.bfloat16)
    return current


def solution(mesh):
    placed = (P("row", "col", None), P(), P(), P(), P(), P(), P(), P(), P())
    return jax.shard_map(
        shards, mesh=mesh, in_specs=placed, out_specs=P("row", "col", None), check_vma=False
    )
```

profile of v0, /device:TPU:1, one launch (start us, length us, event | category | flops | bytes accessed | tf_op | source)
XLA Modules:
  0.0 511.0 jit_solution(10029208373081971723)
XLA Ops:
  6.5 0.7 convert_element_type.43
  7.2 0.1 dynamic_slice.9
  7.3 0.1 dynamic_slice.10
  7.4 1.2 convert_reduce_fusion
  8.5 0.1 copy.70
  8.6 0.1 copy.71
  8.7 1.3 fusion.13
  10.0 0.1 copy.72
  10.1 0.1 copy.73
  10.2 0.1 broadcast_multiply_fusion
  10.3 0.8 slice_bitcast_fusion.2
  11.0 1.3 fusion.16
  12.3 1.3 fusion.39
  13.6 1.1 fusion.28
  14.8 0.0 all-gather.6.cloned.1.call-update
  14.8 0.0 all-gather.8.cloned.1.call-start
  14.8 0.7 all-gather.8.cloned.1.call-update
  15.5 0.0 copy-start.3
  15.5 0.0 copy-start.4
  15.6 0.0 copy-start.5
  15.6 42.0 %all-gather.6.cloned.1.call-done = bf16[512,16,128]{2,1,0:T(8,128)(2,1)} async-done(((bf16[64,16,128]{2,1,0:T(8,128)(2,1)}), bf16[512,16,128]{2,1,0:T(8,128)(2,1)}) %all-gather.6.cloned.1.call-update) | async-done | bytes 2097168 | tf_op jit(solution)/shard_map/all_gather | solution.py:35
  57.5 15.1 %all-to-all-start = ((bf16[512,16,128]{2,1,0:T(8,128)(2,1)}), bf16[512,16,128]{2,1,0:T(8,128)(2,1)S(1)}, u32[]{:S(2)}, u32[]{:S(2)}) async-start(bf16[512,16,128]{2,1,0:T(8,128)(2,1)} %all-gather.6.cloned.1.call-done), calls=%async_computation | async-start | bytes 4194304 | tf_op jit(solution)/shard_map/all_to_all | solution.py:40
  72.6 0.0 all-gather.12.cloned.1.call-start
  72.7 0.3 fusion.5
  73.0 58.1 %all-to-all-done = bf16[512,16,128]{2,1,0:T(8,128)(2,1)S(1)} async-done(((bf16[512,16,128]{2,1,0:T(8,128)(2,1)}), bf16[512,16,128]{2,1,0:T(8,128)(2,1)S(1)}, u32[]{:S(2)}, u32[]{:S(2)}) %all-to-all-start) | async-done | bytes 2097184 | tf_op jit(solution)/shard_map/all_to_all | solution.py:40
  131.1 1.9 copy.74
  133.0 3.4 copy.75
  136.4 61.0 %all-gather.8.cloned.1.call-done = bf16[64,512,128]{2,1,0:T(8,128)(2,1)} async-done(((bf16[64,16,128]{2,1,0:T(8,128)(2,1)}), bf16[64,512,128]{2,1,0:T(8,128)(2,1)}) %all-gather.8.cloned.1.call-update) | async-done | bytes 8388624 | tf_op jit(solution)/shard_map/all_gather | solution.py:46
  197.4 29.2 %copy.76 = bf16[64,512,128]{0,1,2:T(8,128)(2,1)} copy(bf16[64,512,128]{2,1,0:T(8,128)(2,1)} %all-gather.8.cloned.1.call-done) | data formatting | bytes 16777216 | tf_op jit(solution)/shard_map/all_gather | solution.py:46
  226.6 7.0 %fusion.51 = (f32[64,16]{0,1:T(8,128)S(1)}, f32[64,16,128]{0,1,2:T(8,128)S(1)}) fusion(bf16[16,512,128]{1,0,2:T(8,128)(2,1)S(1)} %copy.75, bf16[64,512,128]{0,1,2:T(8,128)(2,1)} %copy.76), kind=kOutput, calls=%fused_computation.91 | convolution fusion | flops 134347776 | bytes 11014144 | tf_op jit(solution)/shard_map/ikc,jkc->ijc/dot_general | solution.py:44
  233.7 0.0 copy-start
  233.7 0.0 copy-start.2
  233.7 0.2 multiply_reduce_fusion.1
  233.9 0.3 add_convert_fusion.1
  234.2 0.0 copy-start.1
  234.3 0.6 copy.77
  234.9 0.4 fusion.52
  235.2 0.1 copy.78
  235.3 0.1 copy.79
  235.4 0.4 multiply_reduce_fusion.2
  235.8 0.1 copy.80
  235.8 0.1 copy.81
  235.9 0.4 add_convert_fusion.2
  236.3 0.4 fusion.37
  236.7 1.1 fusion.18
  237.8 0.0 all-gather.12.cloned.1.call-update
  237.8 34.9 %all-gather.12.cloned.1.call-done = bf16[512,16,128]{2,1,0:T(8,128)(2,1)} async-done(((bf16[64,16,128]{2,1,0:T(8,128)(2,1)}), bf16[512,16,128]{2,1,0:T(8,128)(2,1)}) %all-gather.12.cloned.1.call-update) | async-done | bytes 2097168 | tf_op jit(solution)/shard_map/all_gather | solution.py:35
  272.7 15.1 %all-to-all-start.1 = ((bf16[512,16,128]{2,1,0:T(8,128)(2,1)}), bf16[512,16,128]{2,1,0:T(8,128)(2,1)S(1)}, u32[]{:S(2)}, u32[]{:S(2)}) async-start(bf16[512,16,128]{2,1,0:T(8,128)(2,1)} %all-gather.12.cloned.1.call-done), calls=%async_computation.1 | async-start | bytes 4194304 | tf_op jit(solution)/shard_map/all_to_all | solution.py:40
  287.8 0.0 all-gather.10.cloned.1.call-start
  287.8 0.5 all-gather.10.cloned.1.call-update
  288.4 0.2 all-gather.14.cloned.1.call-start
  288.6 49.3 %all-to-all-done.1 = bf16[512,16,128]{2,1,0:T(8,128)(2,1)S(1)} async-done(((bf16[512,16,128]{2,1,0:T(8,128)(2,1)}), bf16[512,16,128]{2,1,0:T(8,128)(2,1)S(1)}, u32[]{:S(2)}, u32[]{:S(2)}) %all-to-all-start.1) | async-done | bytes 2097184 | tf_op jit(solution)/shard_map/all_to_all | solution.py:40
  337.9 0.5 copy.82
  338.5 1.2 copy.86
  339.7 0.0 all-gather.14.cloned.1.call-update
  339.7 0.3 fusion.2
  340.0 0.0 all-gather.10.cloned.1.call-done
  340.0 3.9 copy.84
  344.0 151.3 %all-gather.14.cloned.1.call-done = bf16[64,512,128]{0,1,2:T(8,128)(2,1)} async-done(((bf16[64,16,128]{0,1,2:T(8,128)(2,1)}), bf16[64,512,128]{0,1,2:T(8,128)(2,1)}) %all-gather.14.cloned.1.call-update) | async-done | bytes 8388624 | tf_op jit(solution)/shard_map/all_gather | solution.py:46
  495.3 7.0 %fusion.53 = (f32[64,16]{0,1:T(8,128)S(1)}, f32[64,16,128]{0,1,2:T(8,128)S(1)}) fusion(bf16[512,16,128]{0,1,2:T(8,128)(2,1)S(1)} %copy.84, bf16[64,512,128]{0,1,2:T(8,128)(2,1)} %all-gather.14.cloned.1.call-done), kind=kOutput, calls=%fused_computation.93 | convolution fusion | flops 134347776 | bytes 11014144 | tf_op jit(solution)/shard_map/ikc,jkc->ijc/dot_general | solution.py:44
  502.4 0.2 multiply_reduce_fusion
  502.6 0.3 add_convert_fusion
  502.9 0.6 copy.85
  503.5 0.9 fusion.8
  (17 shorter events, 0.1 us)
Async XLA Ops:
  6.5 51.0 %all-gather.6.cloned.1.call-start = ((), (), s32[]{:S(2)}) async-start(), calls=%async_computation.2 | async-start | bytes 2359296 | tf_op jit(solution)/shard_map/all_gather | solution.py:35
  14.8 182.6 %all-gather.8.cloned.1.call-start = ((), (), s32[]{:S(2)}) async-start(), calls=%async_computation.3 | async-start | bytes 8650752 | tf_op jit(solution)/shard_map/all_gather | solution.py:46
  15.5 57.1 %copy-start.3 = (f32[2,128]{1,0:T(2,128)S(1)}, f32[2,128]{1,0:T(2,128)}, u32[]{:S(2)}) copy-start(f32[2,128]{1,0:T(2,128)} %param.16) | copy-start | bytes 3076
  15.5 57.1 %copy-start.4 = (f32[2,128]{1,0:T(2,128)S(1)}, f32[2,128]{1,0:T(2,128)}, u32[]{:S(2)}) copy-start(f32[2,128]{1,0:T(2,128)} %param.15) | copy-start | bytes 3076
  15.6 57.1 %copy-start.5 = (bf16[2,128,128]{2,1,0:T(8,128)(2,1)S(1)}, bf16[2,128,128]{2,1,0:T(8,128)(2,1)}, u32[]{:S(2)}) copy-start(bf16[2,128,128]{2,1,0:T(8,128)(2,1)} %param.14) | copy-start | bytes 196612
  57.5 73.5 %all-to-all-start = ((bf16[512,16,128]{2,1,0:T(8,128)(2,1)}), bf16[512,16,128]{2,1,0:T(8,128)(2,1)S(1)}, u32[]{:S(2)}, u32[]{:S(2)}) async-start(bf16[512,16,128]{2,1,0:T(8,128)(2,1)} %all-gather.6.cloned.1.call-done), calls=%async_computation | async-start | bytes 4194304 | tf_op jit(solution)/shard_map/all_to_all | solution.py:40
  72.6 200.1 %all-gather.12.cloned.1.call-start = ((), (), s32[]{:S(2)}) async-start(), calls=%async_computation.5 | async-start | bytes 2359296 | tf_op jit(solution)/shard_map/all_gather | solution.py:35
  233.7 1.2 copy-start
  233.7 1.2 copy-start.2
  234.2 2.0 copy-start.1
  272.7 65.2 %all-to-all-start.1 = ((bf16[512,16,128]{2,1,0:T(8,128)(2,1)}), bf16[512,16,128]{2,1,0:T(8,128)(2,1)S(1)}, u32[]{:S(2)}, u32[]{:S(2)}) async-start(bf16[512,16,128]{2,1,0:T(8,128)(2,1)} %all-gather.12.cloned.1.call-done), calls=%async_computation.1 | async-start | bytes 4194304 | tf_op jit(solution)/shard_map/all_to_all | solution.py:40
  287.8 52.3 %all-gather.10.cloned.1.call-start = ((), (), s32[]{:S(2)}) async-start(), calls=%async_computation.4 | async-start | bytes 2359296 | tf_op jit(solution)/shard_map/all_gather | solution.py:35
  288.4 206.9 %all-gather.14.cloned.1.call-start = ((), (), s32[]{:S(2)}) async-start(), calls=%async_computation.6 | async-start | bytes 17301504 | tf_op jit(solution)/shard_map/all_gather | solution.py:46
Sparse Core Ops, SparseCore 0:
  14.9 42.5 all-gather.5
  60.1 137.2 all-gather.7
  238.0 34.7 all-gather.11
  290.1 44.5 all-gather.9
  339.8 155.4 all-gather.13
where the time goes:
time: 511 us
  waiting for transfers between devices  398 us (78%)
  local copies, waits for them, and re-layouts  42.9 us (8%)
  starting transfers between devices  30.5 us (6%)
  matrix products  17.7 us (3%)
  between operations  13.4 us (3%)
  other arithmetic  8.6 us (2%)
    all_gather x2, waiting for transfers between devices, panel_product(): lax.all_gather(left, 'col', axis=1, tiled=True)  212 us
    all_to_all x2, waiting for transfers between devices, regroup_cols(): lax.all_to_all(gathered, 'col', split_axis=0, concat_axis=1, tiled=True)  107 us
    all_gather x3, waiting for transfers between devices, collect_rows(): return lax.all_gather(tile, 'row', axis=0, tiled=True)  76.9 us
    all_to_all x2, starting transfers between devices, regroup_cols(): lax.all_to_all(gathered, 'col', split_axis=0, concat_axis=1, tiled=True)  30.1 us
    all_gather x1, local copies, waits for them, and re-layouts, panel_product(): lax.all_gather(left, 'col', axis=1, tiled=True)  29.2 us
    dot_general x2, matrix products, panel_product(): jnp.einsum('ikc,jkc->ijc', lax.all_gather(left, 'col', axis=1, tiled=True...  14.1 us
  transfers between devices with their start and end apart: 7, of which 6 were waited for; matrix products, arithmetic and copies ran while one was open for 2% of the time, Pallas kernels for 0%

commit v1 on v0

v1 whole, which is shorter than its diff:
```python
import jax
import jax.numpy as jnp
from jax import lax
from jax.experimental import pallas as pl
from jax.experimental.pallas import tpu as pltpu
from jax.sharding import PartitionSpec as P

MESH = pl.DeviceIdType.MESH
F32 = jnp.float32
BF16 = jnp.bfloat16
ROWS, COLS = 8, 32
TR, TC = 64, 16
CH = 128
POS = TR * TC


def kernel(
    pair_hbm, mask_hbm, gain_hbm, bias_hbm, wp_hbm, wg_hbm, ogain_hbm, obias_hbm, wo_hbm,
    out_ref,
    pair_ref, mask_in, gain_ref, bias_ref, wp_ref, wg_ref, ogain_ref, obias_ref, wo_ref,
    wide, cur, gate, stage, masks, means, rstds, normed, wpt, wgt, wot, gains,
    tile, recv1, recv2, back1, back2, swap1, swap2, mine_r, mine_l, outgoing,
    load_sem, hop_sem, send_sem, in_sem, swap_send, swap_recv, ret_send, ret_recv,
):
    row = lax.axis_index("row")
    col = lax.axis_index("col")
    core = lax.rem(col, 2)
    sibling = col + 1 - 2 * core
    x, y_lo = lax.rem(row, 4), row // 4
    z, y_hi = col // 4, lax.rem(col // 2, 2)

    def diagonal(depth):
        return lax.rem(x - depth + 8, 4)

    def channel_of(depth):
        key = diagonal(depth)
        return (lax.rem(key, 2) * 4 + key // 2 * 2 + y_lo) * 16 + depth * 2 + y_hi

    own = channel_of(z)
    colour_here = lax.rem(diagonal(z), 2)
    loads = [
        pltpu.make_async_copy(src, dst, load_sem.at[n])
        for n, (src, dst) in enumerate([
            (pair_hbm, pair_ref), (mask_hbm, mask_in), (gain_hbm, gain_ref), (bias_hbm, bias_ref), (wp_hbm, wp_ref),
            (wg_hbm, wg_ref), (ogain_hbm, ogain_ref), (obias_hbm, obias_ref), (wo_hbm, wo_ref),
        ])
    ]
    for load in loads:
        load.start()

    barrier = pltpu.get_barrier_semaphore()

    @pl.loop(1, ROWS)
    def _(d):
        pl.semaphore_signal(barrier, inc=1, device_id=(lax.rem(row + d, ROWS), col), device_id_type=MESH)

    @pl.loop(1, COLS)
    def _(d):
        pl.semaphore_signal(barrier, inc=1, device_id=(row, lax.rem(col + d, COLS)), device_id_type=MESH)

    def second_hop():
        pl.semaphore_wait(barrier, ROWS - 1 + COLS - 1)

        @pl.loop(1, COLS)
        def _(d):
            pl.semaphore_signal(hop_sem, inc=1, device_id=(row, lax.rem(col + d, COLS)), device_id_type=MESH)

    order = [(b, g, e) for b in range(2) for g in range(4) for e in range(2)]

    def make_masks():
        lane = lax.broadcasted_iota(jnp.int32, (8, CH), 1)
        mask = mask_in[...].astype(F32)
        number = lax.broadcasted_iota(jnp.int32, (8, 512), 1)
        sub = lax.broadcasted_iota(jnp.int32, (8, 512), 0)
        even_b = jnp.sum(jnp.where(number == TC * col + 2 * sub, mask, 0.0), axis=1, keepdims=True)
        odd_b = jnp.sum(jnp.where(number == TC * col + 2 * sub + 1, mask, 0.0), axis=1, keepdims=True)
        mask_b = jnp.where(lane < 64, even_b, odd_b)
        lane_n = lax.broadcasted_iota(jnp.int32, (512, CH), 1)
        row_n = lax.broadcasted_iota(jnp.int32, (512, CH), 0)
        a_of = ((lane_n // 16) % 4) * 16 + ((lane_n // 8) % 2) + 2 * (lane_n % 8)
        pick = jnp.where(row_n == TR * row + a_of, 1.0, 0.0).astype(BF16)
        mask_a = jnp.dot(jnp.broadcast_to(mask, (8, 512)).astype(BF16), pick, preferred_element_type=F32)
        masks[...] = mask_a * mask_b

    def spread_out(ref, layer, n):
        gains[layer, n] = jnp.broadcast_to(ref[layer : layer + 1, :], (CH, CH)).T

    def prepare(layer):
        turned = wp_ref[layer].astype(F32).T.astype(BF16)
        for g in range(8):
            for q in range(4):
                wpt[layer, g, 16 * q : 16 * q + 16, :] = turned[128 * q + 16 * g : 128 * q + 16 * g + 16]
        spread_out(gain_ref, layer, 0)
        spread_out(bias_ref, layer, 1)

    def prepare_out(layer):
        wgt[layer] = wg_ref[layer].astype(F32).T.astype(BF16)
        wot[layer] = wo_ref[layer].astype(F32).T.astype(BF16)
        spread_out(ogain_ref, layer, 2)
        spread_out(obias_ref, layer, 3)

    def normalize(layer, s, values):
        center = values - jnp.mean(values, axis=0, keepdims=True)
        spread = jnp.mean(center * center, axis=0, keepdims=True)
        scaled = center * lax.rsqrt(spread + 1e-05) * gains[layer, 0] + gains[layer, 1]
        normed[:, CH * s : CH * s + CH] = scaled.astype(BF16)
        cur[s] = values

    def send(src, dst, to_row, to_col, send_sem, recv_sem, here):
        def local():
            pltpu.make_async_copy(src, dst, recv_sem).start()

        def remote():
            pltpu.make_async_remote_copy(
                src_ref=src, dst_ref=dst, send_sem=send_sem, recv_sem=recv_sem,
                device_id=(to_row, to_col), device_id_type=MESH,
            ).start()

        if here is None:
            remote()
        else:
            pl.when(here)(local)
            pl.when(jnp.logical_not(here))(remote)

    def sent(buffer, sem, home):
        count = buffer.shape[0]

        @pl.when(home)
        def _():
            part = buffer.at[pl.ds(0, count - 1)]
            pltpu.make_async_copy(part, part, sem).wait()

        @pl.when(jnp.logical_not(home))
        def _():
            pltpu.make_async_copy(buffer, buffer, sem).wait()

    def arrived(buffer, sem):
        pltpu.make_async_copy(buffer, buffer, sem).wait()

    def scatter(layer):
        to_core = y_lo if layer == 0 else col // 16
        slot = x * COLS + col if layer == 0 else row * 16 + lax.rem(col, 16)
        dst = (recv1 if layer == 0 else recv2).at[slot]
        depths = [lax.rem(z + d, 8) for d in range(8)]
        lows = [y_lo, 1 - y_lo]
        highs = [y_hi, 1 - y_hi]

        def key_of(depth, colour, turn):
            return colour + 2 * lax.rem(diagonal(depth) // 2 + turn // 2, 2)

        @pl.loop(0, 8)
        def _(g):
            colour, turn = g // 4, lax.rem(g, 4)
            key = key_of(z, colour, turn)
            low = lax.rem(y_lo + turn, 2)
            block = colour * 4 + key // 2 * 2 + low
            proj = jnp.dot(wpt[layer, block], normed[...], preferred_element_type=F32)
            left = jax.nn.sigmoid(proj[0:16]) * proj[16:32]
            right = jax.nn.sigmoid(proj[32:48]) * proj[48:64]
            for s in range(8):
                keep = masks[s : s + 1, :]
                stage[pl.ds(s, 16, stride=16), :] = left[:, CH * s : CH * s + CH] * keep
                stage[pl.ds(s + 8, 16, stride=16), :] = right[:, CH * s : CH * s + CH] * keep
            first = block * 16
            tile[pl.ds(first, 16)] = stage[0:256, :].reshape(16, 16, CH).astype(BF16)
            to_rows = [low * 4 + lax.rem(key + z + d, 4) for d in range(4)]

            def direct(dz, dh, here=None):
                send(
                    tile.at[first + depths[dz] * 2 + highs[dh]], dst,
                    to_rows[dz % 4], depths[dz] * 4 + highs[dh] * 2 + to_core,
                    send_sem.at[layer], in_sem.at[layer], here,
                )

            for n, (dh, dz) in enumerate([(dh, dz) for dh in range(2) for dz in (0, 3, 6, 1, 4, 7, 2, 5)]):
                here = jnp.logical_and(g == 4 * colour_here, to_core == core) if n == 0 else None
                direct(dz, dh, here)

        return to_core == core

    def make_gate(layer):
        for s in range(8):
            part = jnp.dot(wgt[layer], normed[:, CH * s : CH * s + CH], preferred_element_type=F32)
            gate[s] = jax.nn.sigmoid(part)

    def merge(first, second):
        low = lax.broadcasted_iota(jnp.int32, first.shape, 2) < 64
        even = jnp.where(low, first, pltpu.roll(second, 64, 2))
        odd = jnp.where(low, pltpu.roll(first, 64, 2), second)
        return even, odd

    def gather(layer):
        recv, width, pairs = (recv1, 32, 2) if layer == 0 else (recv2, 16, 4)
        for p in range(pairs):
            first = recv[2 * p * width : (2 * p + 1) * width].astype(F32)
            second = recv[(2 * p + 1) * width : (2 * p + 2) * width].astype(F32)
            even, odd = merge(first, second)
            left = jnp.concatenate([even[:, :8], odd[:, :8]], axis=1).reshape(width * 16, CH)
            right = jnp.concatenate([even[:, 8:], odd[:, 8:]], axis=1).reshape(width * 16, CH)
            if layer == 0:
                mine_l[0:512, 128 * p : 128 * p + 128] = left.astype(BF16)
                mine_r[128 * p : 128 * p + 128, :] = right.T.astype(BF16)
            else:
                mine_l[512:768, 128 * p : 128 * p + 128] = left.astype(BF16)
                mine_r[:, 128 * p : 128 * p + 128] = right.astype(BF16)

    def quadrant(layer, q, right, dst):
        if layer == 0:
            mixed = jnp.dot(right, mine_l[0:512, 0:256], preferred_element_type=F32)
        else:
            mixed = lax.dot_general(right, mine_l[512:768, :], (((1,), (1,)), ((), ())), preferred_element_type=F32)
        for p in range(2):
            block = mixed[:, 128 * p : 128 * p + 128].reshape(16, 16, CH)
            even, odd = merge(block[:, :8], block[:, 8:])
            base = q * 64 + p * 32
            outgoing[base : base + 16] = even.astype(BF16)
            outgoing[base + 16 : base + 32] = odd.astype(BF16)
        side = core if q == 0 else 1 - core
        z_low = lax.rem(z, 4)
        cells = [
            (dz, lax.rem(z_low + dz, 4) * 4 + (y_hi if dy == 0 else 1 - y_hi) * 2 + (core if dc == 0 else 1 - core))
            for dy in range(2) for dc in range(2) for dz in (0, 2, 1, 3)
        ]

        @pl.loop(0, 4)
        def _(d):
            lines = [lax.rem(x + d + n, 4) for n in range(4)]
            for n, (dz, cell) in enumerate(cells):
                r = lines[dz]
                here = None
                if n == 0:
                    here = jnp.logical_and(d == 0, jnp.logical_and(y_lo == core, z // 4 == side))
                src = outgoing.at[q * 64 + r * 16 + cell]

                send(
                    src, dst, core * 4 + r, side * 16 + cell,
                    ret_send.at[layer], ret_recv.at[2 * layer + colour_here], here,
                )

    def multiply(layer):
        back = (back1 if layer == 0 else back2).at[own]
        swap = swap1 if layer == 0 else swap2
        gather(layer)
        exchange = pltpu.make_async_remote_copy(
            src_ref=mine_r, dst_ref=swap, send_sem=swap_send.at[layer], recv_sem=swap_recv.at[layer],
            device_id=(row, sibling), device_id_type=MESH,
        )
        exchange.start()
        quadrant(layer, 0, mine_r[...], back)
        exchange.wait_recv()
        quadrant(layer, 1, swap[...], back)
        exchange.wait_send()

    def finish(layer):
        back = back1 if layer == 0 else back2
        halves = []
        for colour in range(2):
            arrived(back.at[pl.ds(64 * colour, 64)], ret_recv.at[2 * layer + colour])
            total = jnp.zeros((8, CH), F32)
            for g in range(4 * colour, 4 * colour + 4):
                part = back[16 * g : 16 * g + 16].astype(F32)
                wide[128 * g : 128 * g + 128, :] = part.reshape(128, CH)
                total = total + jnp.sum(part, axis=0)
            mean = total * (1.0 / 64)
            total = jnp.zeros((8, CH), F32)
            for g in range(4 * colour, 4 * colour + 4):
                part = wide[128 * g : 128 * g + 128, :].reshape(16, 8, CH) - mean[None]
                total = total + jnp.sum(part * part, axis=0)
            halves.append((mean, total))
        (mean0, total0), (mean1, total1) = halves
        apart = 0.5 * (mean0 - mean1)
        means[...] = 0.5 * (mean0 + mean1)
        rstds[...] = lax.rsqrt((total0 + total1) * (1.0 / CH) + apart * apart + 1e-05)

    def updated(layer, s):
        mixed = wide[pl.ds(s, CH, stride=8), :]
        out_normed = (mixed - means[s : s + 1, :]) * rstds[s : s + 1, :] * gains[layer, 2] + gains[layer, 3]
        update = jnp.dot(wot[layer], out_normed.astype(BF16), preferred_element_type=F32)
        return cur[s] + gate[s] * update

    for load in loads:
        load.wait()
    prepare(0)
    make_masks()
    second_hop()
    wide[...] = pair_ref[...].astype(F32).reshape(POS, CH)
    for s in range(8):
        rows = [wide[pl.ds(256 * g + 16 * e + 2 * s + b, 8, stride=32), :] for b, g, e in order]
        normalize(0, s, jnp.concatenate(rows, axis=0).T)
    pl.semaphore_wait(hop_sem, COLS - 1)
    home1 = scatter(0)
    prepare_out(0)
    make_gate(0)
    prepare(1)
    prepare_out(1)
    arrived(recv1, in_sem.at[0])
    multiply(0)
    sent(tile, send_sem.at[0], home1)
    finish(0)
    for s in range(8):
        normalize(1, s, updated(0, s).astype(BF16).astype(F32))
    home2 = scatter(1)
    make_gate(1)
    sent(outgoing, ret_send.at[0], home1)
    arrived(recv2, in_sem.at[1])
    multiply(1)
    sent(tile, send_sem.at[1], home2)
    finish(1)
    for s in range(8):
        values = updated(1, s).T
        for n, (b, g, e) in enumerate(order):
            stage[pl.ds(256 * g + 16 * e + 2 * s + b, 8, stride=32), :] = values[8 * n : 8 * n + 8]
    out_ref[...] = stage[...].reshape(TR, TC, CH).astype(BF16)
    sent(outgoing, ret_send.at[1], home1)


def shards(pair, residue_mask, in_gain, in_bias, proj_weight, gate_weight, out_gain, out_bias, out_weight):
    arguments = (
        pair, residue_mask.reshape(1, 512), in_gain, in_bias, proj_weight, gate_weight, out_gain, out_bias, out_weight
    )
    dma = pltpu.SemaphoreType.DMA
    return pl.pallas_call(
        kernel,
        out_shape=pltpu.VMEM((TR, TC, CH), BF16),
        in_specs=[pl.BlockSpec(memory_space=pltpu.HBM)] * 9,
        out_specs=pl.BlockSpec(memory_space=pltpu.VMEM),
        scratch_shapes=[pltpu.VMEM(value.shape, value.dtype) for value in arguments] + [
            pltpu.VMEM((POS, CH), F32),
            pltpu.VMEM((8, CH, CH), F32),
            pltpu.VMEM((8, CH, CH), F32),
            pltpu.VMEM((POS, CH), F32),
            pltpu.VMEM((8, CH), F32),
            pltpu.VMEM((8, CH), F32),
            pltpu.VMEM((8, CH), F32),
            pltpu.VMEM((CH, POS), BF16),
            pltpu.VMEM((2, 8, 64, CH), BF16),
            pltpu.VMEM((2, CH, CH), BF16),
            pltpu.VMEM((2, CH, CH), BF16),
            pltpu.VMEM((2, 4, CH, CH), F32),
            pltpu.VMEM((CH, 16, CH), BF16),
            pltpu.VMEM((CH, 16, CH), BF16),
            pltpu.VMEM((CH, 16, CH), BF16),
            pltpu.VMEM((CH, 8, CH), BF16),
            pltpu.VMEM((CH, 8, CH), BF16),
            pltpu.VMEM((256, 512), BF16),
            pltpu.VMEM((256, 512), BF16),
            pltpu.VMEM((256, 512), BF16),
            pltpu.VMEM((768, 512), BF16),
            pltpu.VMEM((CH, 8, CH), BF16),
            dma((9,)),
            pltpu.SemaphoreType.REGULAR,
            dma((2,)), dma((2,)), dma((2,)), dma((2,)), dma((2,)), dma((4,)),
        ],
        compiler_params=pltpu.CompilerParams(
            collective_id=0, has_side_effects=True, vmem_limit_bytes=48 * 1024 * 1024
        ),
        cost_estimate=pl.CostEstimate(flops=700_000_000, bytes_accessed=4_000_000, transcendentals=1_000_000),
    )(*[pltpu.with_memory_space_constraint(value, pltpu.HBM) for value in arguments])


def solution(mesh):
    placed = (P("row", "col", None), P(), P(), P(), P(), P(), P(), P(), P())
    return jax.shard_map(
        shards, mesh=mesh, in_specs=placed, out_specs=P("row", "col", None), check_vma=False
    )
```

time: 511 us -> 70.9 us (0.14)
  waiting for transfers between devices: 398 us -> 0 us
  Pallas kernels: 0 us -> 70.1 us
  local copies, waits for them, and re-layouts: 42.9 us -> 0.71 us
  starting transfers between devices: 30.5 us -> 0 us
  matrix products: 17.7 us -> 0 us
  between operations: 13.4 us -> 0.01 us
  other arithmetic: 8.6 us -> 0 us
    all_gather x5 -> x0, waiting for transfers between devices: 289 us -> none  [the longest x2 212 us: panel_product(): lax.all_gather(left, 'col', axis=1, tiled=True)]
    all_to_all x2 -> x0, waiting for transfers between devices: 107 us -> none  [regroup_cols(): lax.all_to_all(gathered, 'col', split_axis=0, concat_axis=1, tiled=True)]
    pallas_call x0 -> x1, Pallas kernels: none -> 70.1 us  [shards(): pl.pallas_call(kernel, out_shape=pltpu.VMEM((TR, TC, CH), BF16), in_specs...]
    all_gather x2 -> x0, local copies, waits for them, and re-layouts: 33.1 us -> none  [the longest x1 29.2 us: panel_product(): lax.all_gather(left, 'col', axis=1, tiled=True)]
    all_to_all x2 -> x0, starting transfers between devices: 30.1 us -> none  [regroup_cols(): lax.all_to_all(gathered, 'col', split_axis=0, concat_axis=1, tiled=True)]
    dot_general x8 -> x0, matrix products: 17.7 us -> none  [the longest x2 14.1 us: panel_product(): jnp.einsum('ikc,jkc->ijc', lax.all_gather(left, 'col', axis=1, tiled=True...]
    all_to_all x3 -> x0, local copies, waits for them, and re-layouts: 5.85 us -> none  [regroup_cols(): lax.all_to_all(gathered, 'col', split_axis=0, concat_axis=1, tiled=True)]
    convert_element_type x7 -> x0, other arithmetic: 5.23 us -> none  [the longest x2 2.23 us: factors(): (jax.nn.sigmoid(proj[..., :hidden]) * proj[..., hidden:2 * hidden] * mask...]
  transfers between devices with their start and end apart: 7 -> 0, of which waited for: 6 -> 0; matrix products, arithmetic and copies ran while one was open for 2% -> 0% of each run, Pallas kernels for 0% -> 0%
where the time goes in v1:
time: 70.9 us; the launch traced here: 70.8 us
  Pallas kernels  70.1 us (99%)
  local copies, waits for them, and re-layouts  0.71 us (1%)
    pallas_call x1, Pallas kernels, shards(): pl.pallas_call(kernel, out_shape=pltpu.VMEM((TR, TC, CH), BF16), in_specs...  70.1 us

profile of v1, /device:TPU:1, one launch (start us, length us, event | category | flops | bytes accessed | tf_op | source)
XLA Modules:
  0.0 70.8 jit_solution(8173819194166441718)
XLA Ops:
  0.0 70.1 %shard_map.91 = bf16[64,16,128]{2,1,0:T(8,128)(2,1)S(1)} custom-call(bf16[64,16,128]{2,1,0:T(8,128)(2,1)} %pair_hbm.1, s32[1,512]{1,0:T(1,128)} %bitcast.1, f32[2,128]{1,0:T(2,128)} %gain_hbm.1, f32[2,128]{1,0:T(2,128)} %bias_hbm.1, bf16[2,128,512]{2,1,0:T(8,128)(2,1)} %wp_hbm.1, bf16[2,128,128]{2,1,0:T(8,128)(2,1)} %wg_hbm.1, f32[2,128]{1,0:T(2,128)} %ogain_hbm.1, ...), custom_call_target="tpu_custom_call" | custom-call | flops 700000000 | bytes 4000000 | tf_op jit(solution)/shard_map/pallas_call | solution.py:322
  70.1 0.7 copy.11

commit v2 on v1

--- a/solution.py
+++ b/solution.py
@@ -19,7 +19,7 @@
     out_ref,
     pair_ref, mask_in, gain_ref, bias_ref, wp_ref, wg_ref, ogain_ref, obias_ref, wo_ref,
     wide, cur, gate, stage, masks, means, rstds, normed, wpt, wgt, wot, gains,
-    tile, recv1, recv2, back1, back2, swap1, swap2, mine_r, mine_l, outgoing,
+    tile, recv1, recv2, back1, back2, swap1, swap2, mine_r, mine_l, mine_l2, raw_r, outgoing,
     load_sem, hop_sem, send_sem, in_sem, swap_send, swap_recv, ret_send, ret_recv,
 ):
     row = lax.axis_index("row")
@@ -29,15 +29,10 @@
     x, y_lo = lax.rem(row, 4), row // 4
     z, y_hi = col // 4, lax.rem(col // 2, 2)
 
-    def diagonal(depth):
-        return lax.rem(x - depth + 8, 4)
-
-    def channel_of(depth):
-        key = diagonal(depth)
-        return (lax.rem(key, 2) * 4 + key // 2 * 2 + y_lo) * 16 + depth * 2 + y_hi
-
-    own = channel_of(z)
-    colour_here = lax.rem(diagonal(z), 2)
+    colour_here = lax.rem(x + z, 2)
+    own = (colour_here * 8 + z) * 8 + x // 2 * 4 + y_hi * 2 + y_lo
+    z_low = lax.rem(z, 4)
+
     loads = [
         pltpu.make_async_copy(src, dst, load_sem.at[n])
         for n, (src, dst) in enumerate([
@@ -86,10 +81,10 @@
         gains[layer, n] = jnp.broadcast_to(ref[layer : layer + 1, :], (CH, CH)).T
 
     def prepare(layer):
-        turned = wp_ref[layer].astype(F32).T.astype(BF16)
-        for g in range(8):
-            for q in range(4):
-                wpt[layer, g, 16 * q : 16 * q + 16, :] = turned[128 * q + 16 * g : 128 * q + 16 * g + 16]
+        turned = wp_ref[layer].astype(F32).T
+        for b in range(16):
+            rows = [turned[128 * q + 8 * b : 128 * q + 8 * b + 8] for q in range(4)]
+            wpt[layer, b] = jnp.concatenate(rows, axis=0).astype(BF16)
         spread_out(gain_ref, layer, 0)
         spread_out(bias_ref, layer, 1)
 
@@ -139,42 +134,41 @@
 
     def scatter(layer):
         to_core = y_lo if layer == 0 else col // 16
-        slot = x * COLS + col if layer == 0 else row * 16 + lax.rem(col, 16)
+        corner = y_hi * 2 + core
+        slot = z * 16 + x * 4 + corner if layer == 0 else z_low * 32 + row * 4 + corner
         dst = (recv1 if layer == 0 else recv2).at[slot]
-        depths = [lax.rem(z + d, 8) for d in range(8)]
         lows = [y_lo, 1 - y_lo]
         highs = [y_hi, 1 - y_hi]
-
-        def key_of(depth, colour, turn):
-            return colour + 2 * lax.rem(diagonal(depth) // 2 + turn // 2, 2)
+        halves = [x // 2, 1 - x // 2]
 
         @pl.loop(0, 8)
         def _(g):
-            colour, turn = g // 4, lax.rem(g, 4)
-            key = key_of(z, colour, turn)
-            low = lax.rem(y_lo + turn, 2)
-            block = colour * 4 + key // 2 * 2 + low
-            proj = jnp.dot(wpt[layer, block], normed[...], preferred_element_type=F32)
-            left = jax.nn.sigmoid(proj[0:16]) * proj[16:32]
-            right = jax.nn.sigmoid(proj[32:48]) * proj[48:64]
+            colour, step = g // 4, lax.rem(g, 4)
+            depths = [lax.rem(z + 4 + step, 8), lax.rem(z + 3 - step, 8)]
+            blocks = [colour * 8 + depth for depth in depths]
+            weights = jnp.concatenate([wpt[layer, block] for block in blocks], axis=0)
+            proj = jnp.dot(weights, normed[...], preferred_element_type=F32)
+            left = jnp.concatenate([jax.nn.sigmoid(proj[n : n + 8]) * proj[n + 8 : n + 16] for n in (0, 32)], axis=0)
+            right = jnp.concatenate([jax.nn.sigmoid(proj[n : n + 8]) * proj[n + 8 : n + 16] for n in (16, 48)], axis=0)
             for s in range(8):
                 keep = masks[s : s + 1, :]
                 stage[pl.ds(s, 16, stride=16), :] = left[:, CH * s : CH * s + CH] * keep
                 stage[pl.ds(s + 8, 16, stride=16), :] = right[:, CH * s : CH * s + CH] * keep
-            first = block * 16
-            tile[pl.ds(first, 16)] = stage[0:256, :].reshape(16, 16, CH).astype(BF16)
-            to_rows = [low * 4 + lax.rem(key + z + d, 4) for d in range(4)]
-
-            def direct(dz, dh, here=None):
-                send(
-                    tile.at[first + depths[dz] * 2 + highs[dh]], dst,
-                    to_rows[dz % 4], depths[dz] * 4 + highs[dh] * 2 + to_core,
-                    send_sem.at[layer], in_sem.at[layer], here,
-                )
-
-            for n, (dh, dz) in enumerate([(dh, dz) for dh in range(2) for dz in (0, 3, 6, 1, 4, 7, 2, 5)]):
-                here = jnp.logical_and(g == 4 * colour_here, to_core == core) if n == 0 else None
-                direct(dz, dh, here)
+            for n, block in enumerate(blocks):
+                tile[pl.ds(block * 8, 8)] = stage[128 * n : 128 * n + 128, :].reshape(8, 16, CH).astype(BF16)
+            odd = [lax.rem(colour + depth, 2) for depth in depths]
+            for dx in (1, 0):
+                for dh in (1, 0):
+                    for dl in (1, 0):
+                        for n in range(2):
+                            here = None
+                            if n == 1 and dx + dh + dl == 0:
+                                here = jnp.logical_and(g == 4 * colour_here + 3, to_core == core)
+                            send(
+                                tile.at[blocks[n] * 8 + halves[dx] * 4 + highs[dh] * 2 + lows[dl]], dst,
+                                lows[dl] * 4 + halves[dx] * 2 + odd[n], depths[n] * 4 + highs[dh] * 2 + to_core,
+                                send_sem.at[layer], in_sem.at[8 * layer + z], here,
+                            )
 
         return to_core == core
 
@@ -189,26 +183,43 @@
         odd = jnp.where(low, pltpu.roll(first, 64, 2), second)
         return even, odd
 
+    def far_first(step, same):
+        falling = (z_low < 2) == same
+        return jnp.where(falling, 3 - step, step)
+
     def gather(layer):
-        recv, width, pairs = (recv1, 32, 2) if layer == 0 else (recv2, 16, 4)
-        for p in range(pairs):
-            first = recv[2 * p * width : (2 * p + 1) * width].astype(F32)
-            second = recv[(2 * p + 1) * width : (2 * p + 2) * width].astype(F32)
-            even, odd = merge(first, second)
-            left = jnp.concatenate([even[:, :8], odd[:, :8]], axis=1).reshape(width * 16, CH)
-            right = jnp.concatenate([even[:, 8:], odd[:, 8:]], axis=1).reshape(width * 16, CH)
+        for step in range(8 if layer == 0 else 4):
             if layer == 0:
-                mine_l[0:512, 128 * p : 128 * p + 128] = left.astype(BF16)
-                mine_r[128 * p : 128 * p + 128, :] = right.T.astype(BF16)
+                recv, width, pairs = recv1, 16, 2
+                place = lax.rem(z + (4, 5, 3, 6, 2, 7, 1, 0)[step], 8)
+                sem = in_sem.at[place]
             else:
-                mine_l[512:768, 128 * p : 128 * p + 128] = left.astype(BF16)
-                mine_r[:, 128 * p : 128 * p + 128] = right.astype(BF16)
+                recv, width, pairs = recv2, 32, 4
+                place = far_first(step, z // 4 == core)
+                sem = in_sem.at[8 + core * 4 + place]
+            arrived(recv.at[pl.ds(place * width, width)], sem)
+            rows = pl.ds(pl.multiple_of(place * 64, 64), 64)
+            for p in range(pairs):
+                first = recv[pl.ds(place * width + 8 * p, 4)].astype(F32)
+                second = recv[pl.ds(place * width + 8 * p + 4, 4)].astype(F32)
+                even, odd = merge(first, second)
+                left = jnp.concatenate([even[:, :8], odd[:, :8]], axis=1).reshape(64, CH)
+                right = jnp.concatenate([even[:, 8:], odd[:, 8:]], axis=1).reshape(64, CH)
+                if layer == 0:
+                    mine_l[rows, 128 * p : 128 * p + 128] = left.astype(BF16)
+                    raw_r[rows, 128 * p : 128 * p + 128] = right
+                else:
+                    mine_l2[rows, 128 * p : 128 * p + 128] = left.astype(BF16)
+                    mine_r[rows, 128 * p : 128 * p + 128] = right.astype(BF16)
+        if layer == 0:
+            for p in range(2):
+                mine_r[128 * p : 128 * p + 128, :] = raw_r[:, 128 * p : 128 * p + 128].T.astype(BF16)
 
     def quadrant(layer, q, right, dst):
         if layer == 0:
-            mixed = jnp.dot(right, mine_l[0:512, 0:256], preferred_element_type=F32)
+            mixed = jnp.dot(right, mine_l[...], preferred_element_type=F32)
         else:
-            mixed = lax.dot_general(right, mine_l[512:768, :], (((1,), (1,)), ((), ())), preferred_element_type=F32)
+            mixed = lax.dot_general(right, mine_l2[...], (((1,), (1,)), ((), ())), preferred_element_type=F32)
         for p in range(2):
             block = mixed[:, 128 * p : 128 * p + 128].reshape(16, 16, CH)
             even, odd = merge(block[:, :8], block[:, 8:])
@@ -216,26 +227,22 @@
             outgoing[base : base + 16] = even.astype(BF16)
             outgoing[base + 16 : base + 32] = odd.astype(BF16)
         side = core if q == 0 else 1 - core
-        z_low = lax.rem(z, 4)
-        cells = [
-            (dz, lax.rem(z_low + dz, 4) * 4 + (y_hi if dy == 0 else 1 - y_hi) * 2 + (core if dc == 0 else 1 - core))
-            for dy in range(2) for dc in range(2) for dz in (0, 2, 1, 3)
-        ]
+        lines = [lax.rem(x + n, 4) for n in range(4)]
+        corners = [(y_hi if dy == 0 else 1 - y_hi) * 2 + (core if dc == 0 else 1 - core) for dy in range(2) for dc in range(2)]
 
         @pl.loop(0, 4)
-        def _(d):
-            lines = [lax.rem(x + d + n, 4) for n in range(4)]
-            for n, (dz, cell) in enumerate(cells):
-                r = lines[dz]
-                here = None
-                if n == 0:
-                    here = jnp.logical_and(d == 0, jnp.logical_and(y_lo == core, z // 4 == side))
-                src = outgoing.at[q * 64 + r * 16 + cell]
-
-                send(
-                    src, dst, core * 4 + r, side * 16 + cell,
-                    ret_send.at[layer], ret_recv.at[2 * layer + colour_here], here,
-                )
+        def _(step):
+            depth = far_first(step, z // 4 == side)
+            for corner in (3, 2, 1, 0):
+                for dx in (2, 1, 3, 0):
+                    here = None
+                    if corner == 0 and dx == 0:
+                        here = jnp.logical_and(y_lo == core, side * 4 + depth == z)
+                    cell = depth * 4 + corners[corner]
+                    send(
+                        outgoing.at[q * 64 + lines[dx] * 16 + cell], dst, core * 4 + lines[dx], side * 16 + cell,
+                        ret_send.at[layer], ret_recv.at[2 * layer + colour_here], here,
+                    )
 
     def multiply(layer):
         back = (back1 if layer == 0 else back2).at[own]
@@ -289,21 +296,19 @@
         normalize(0, s, jnp.concatenate(rows, axis=0).T)
     pl.semaphore_wait(hop_sem, COLS - 1)
     home1 = scatter(0)
+    multiply(0)
     prepare_out(0)
     make_gate(0)
     prepare(1)
     prepare_out(1)
-    arrived(recv1, in_sem.at[0])
-    multiply(0)
     sent(tile, send_sem.at[0], home1)
     finish(0)
     for s in range(8):
         normalize(1, s, updated(0, s).astype(BF16).astype(F32))
     home2 = scatter(1)
+    sent(outgoing, ret_send.at[0], home1)
+    multiply(1)
     make_gate(1)
-    sent(outgoing, ret_send.at[0], home1)
-    arrived(recv2, in_sem.at[1])
-    multiply(1)
     sent(tile, send_sem.at[1], home2)
     finish(1)
     for s in range(8):
@@ -333,7 +338,7 @@
             pltpu.VMEM((8, CH), F32),
             pltpu.VMEM((8, CH), F32),
             pltpu.VMEM((CH, POS), BF16),
-            pltpu.VMEM((2, 8, 64, CH), BF16),
+            pltpu.VMEM((2, 16, 32, CH), BF16),
             pltpu.VMEM((2, CH, CH), BF16),
             pltpu.VMEM((2, CH, CH), BF16),
             pltpu.VMEM((2, 4, CH, CH), F32),
@@ -345,11 +350,13 @@
             pltpu.VMEM((256, 512), BF16),
             pltpu.VMEM((256, 512), BF16),
             pltpu.VMEM((256, 512), BF16),
-            pltpu.VMEM((768, 512), BF16),
+            pltpu.VMEM((512, 256), BF16),
+            pltpu.VMEM((256, 512), BF16),
+            pltpu.VMEM((512, 256), F32),
             pltpu.VMEM((CH, 8, CH), BF16),
             dma((9,)),
             pltpu.SemaphoreType.REGULAR,
-            dma((2,)), dma((2,)), dma((2,)), dma((2,)), dma((2,)), dma((4,)),
+            dma((2,)), dma((16,)), dma((2,)), dma((2,)), dma((2,)), dma((4,)),
         ],
         compiler_params=pltpu.CompilerParams(
             collective_id=0, has_side_effects=True, vmem_limit_bytes=48 * 1024 * 1024

time: 70.9 us -> 68.7 us (0.969)
  Pallas kernels: 70.1 us -> 67.8 us
    pallas_call x1, Pallas kernels: 70.1 us -> 67.8 us  [shards(): pl.pallas_call(kernel, out_shape=pltpu.VMEM((TR, TC, CH), BF16), in_specs...]
where the time goes in v2:
time: 68.7 us; the launch traced here: 68.6 us
  Pallas kernels  67.8 us (99%)
  local copies, waits for them, and re-layouts  0.71 us (1%)
    pallas_call x1, Pallas kernels, shards(): pl.pallas_call(kernel, out_shape=pltpu.VMEM((TR, TC, CH), BF16), in_specs...  67.8 us

profile of v2, /device:TPU:1, one launch (start us, length us, event | category | flops | bytes accessed | tf_op | source)
XLA Modules:
  0.0 68.6 jit_solution(13835399248283298439)
XLA Ops:
  0.0 67.8 %shard_map.91 = bf16[64,16,128]{2,1,0:T(8,128)(2,1)S(1)} custom-call(bf16[64,16,128]{2,1,0:T(8,128)(2,1)} %pair_hbm.1, s32[1,512]{1,0:T(1,128)} %bitcast.1, f32[2,128]{1,0:T(2,128)} %gain_hbm.1, f32[2,128]{1,0:T(2,128)} %bias_hbm.1, bf16[2,128,512]{2,1,0:T(8,128)(2,1)} %wp_hbm.1, bf16[2,128,128]{2,1,0:T(8,128)(2,1)} %wg_hbm.1, f32[2,128]{1,0:T(2,128)} %ogain_hbm.1, ...), custom_call_target="tpu_custom_call" | custom-call | flops 700000000 | bytes 4000000 | tf_op jit(solution)/shard_map/pallas_call | solution.py:327
  67.9 0.7 %copy.11 = bf16[64,16,128]{2,1,0:T(8,128)(2,1)} copy(bf16[64,16,128]{2,1,0:T(8,128)(2,1)S(1)} %shard_map.91) | data formatting | bytes 524288

commit v3 on v2

--- a/solution.py
+++ b/solution.py
@@ -144,7 +144,8 @@
         @pl.loop(0, 8)
         def _(g):
             colour, step = g // 4, lax.rem(g, 4)
-            depths = [lax.rem(z + 4 + step, 8), lax.rem(z + 3 - step, 8)]
+            ahead = jnp.where(step == 0, 3, jnp.where(step == 1, 4, 4 - step))
+            depths = [lax.rem(z + ahead, 8), lax.rem(z + jnp.where(step == 1, 0, 8 - ahead), 8)]
             blocks = [colour * 8 + depth for depth in depths]
             weights = jnp.concatenate([wpt[layer, block] for block in blocks], axis=0)
             proj = jnp.dot(weights, normed[...], preferred_element_type=F32)
@@ -163,7 +164,7 @@
                         for n in range(2):
                             here = None
                             if n == 1 and dx + dh + dl == 0:
-                                here = jnp.logical_and(g == 4 * colour_here + 3, to_core == core)
+                                here = jnp.logical_and(g == 4 * colour_here + 1, to_core == core)
                             send(
                                 tile.at[blocks[n] * 8 + halves[dx] * 4 + highs[dh] * 2 + lows[dl]], dst,
                                 lows[dl] * 4 + halves[dx] * 2 + odd[n], depths[n] * 4 + highs[dh] * 2 + to_core,
@@ -191,41 +192,32 @@
         for step in range(8 if layer == 0 else 4):
             if layer == 0:
                 recv, width, pairs = recv1, 16, 2
-                place = lax.rem(z + (4, 5, 3, 6, 2, 7, 1, 0)[step], 8)
+                place = lax.rem(z + (5, 3, 4, 0, 6, 2, 7, 1)[step], 8)
                 sem = in_sem.at[place]
             else:
                 recv, width, pairs = recv2, 32, 4
                 place = far_first(step, z // 4 == core)
                 sem = in_sem.at[8 + core * 4 + place]
             arrived(recv.at[pl.ds(place * width, width)], sem)
-            rows = pl.ds(pl.multiple_of(place * 64, 64), 64)
+            rows = pl.ds(64 * step if layer == 0 else pl.multiple_of(place * 64, 64), 64)
             for p in range(pairs):
                 first = recv[pl.ds(place * width + 8 * p, 4)].astype(F32)
                 second = recv[pl.ds(place * width + 8 * p + 4, 4)].astype(F32)
                 even, odd = merge(first, second)
                 left = jnp.concatenate([even[:, :8], odd[:, :8]], axis=1).reshape(64, CH)
                 right = jnp.concatenate([even[:, 8:], odd[:, 8:]], axis=1).reshape(64, CH)
+                lanes = slice(128 * p, 128 * p + 128)
                 if layer == 0:
-                    mine_l[rows, 128 * p : 128 * p + 128] = left.astype(BF16)
-                    raw_r[rows, 128 * p : 128 * p + 128] = right
+                    mine_l[rows, lanes] = left.astype(BF16)
+                    raw_r[rows, lanes] = right
                 else:
-                    mine_l2[rows, 128 * p : 128 * p + 128] = left.astype(BF16)
-                    mine_r[rows, 128 * p : 128 * p + 128] = right.astype(BF16)
-        if layer == 0:
-            for p in range(2):
-                mine_r[128 * p : 128 * p + 128, :] = raw_r[:, 128 * p : 128 * p + 128].T.astype(BF16)
+                    mine_l2[rows, lanes] = left.astype(BF16)
+                    mine_r[rows, lanes] = right.astype(BF16)
+                if layer == 0 and step % 2 == 1:
+                    block = slice(64 * step - 64, 64 * step + 64)
+                    mine_r[lanes, block] = raw_r[block, lanes].T.astype(BF16)
 
     def quadrant(layer, q, right, dst):
-        if layer == 0:
-            mixed = jnp.dot(right, mine_l[...], preferred_element_type=F32)
-        else:
-            mixed = lax.dot_general(right, mine_l2[...], (((1,), (1,)), ((), ())), preferred_element_type=F32)
-        for p in range(2):
-            block = mixed[:, 128 * p : 128 * p + 128].reshape(16, 16, CH)
-            even, odd = merge(block[:, :8], block[:, 8:])
-            base = q * 64 + p * 32
-            outgoing[base : base + 16] = even.astype(BF16)
-            outgoing[base + 16 : base + 32] = odd.astype(BF16)
         side = core if q == 0 else 1 - core
         lines = [lax.rem(x + n, 4) for n in range(4)]
         corners = [(y_hi if dy == 0 else 1 - y_hi) * 2 + (core if dc == 0 else 1 - core) for dy in range(2) for dc in range(2)]
@@ -233,14 +225,25 @@
         @pl.loop(0, 4)
         def _(step):
             depth = far_first(step, z // 4 == side)
+            rows = right[pl.ds(pl.multiple_of(depth * 64, 64), 64), :]
+            if layer == 0:
+                mixed = jnp.dot(rows, mine_l[...], preferred_element_type=F32)
+            else:
+                mixed = lax.dot_general(rows, mine_l2[...], (((1,), (1,)), ((), ())), preferred_element_type=F32)
+            base = q * 64 + depth * 16
+            for p in range(2):
+                block = mixed[:, 128 * p : 128 * p + 128].reshape(4, 16, CH)
+                even, odd = merge(block[:, :8], block[:, 8:])
+                outgoing[pl.ds(base + 8 * p, 4)] = even.astype(BF16)
+                outgoing[pl.ds(base + 8 * p + 4, 4)] = odd.astype(BF16)
             for corner in (3, 2, 1, 0):
                 for dx in (2, 1, 3, 0):
                     here = None
                     if corner == 0 and dx == 0:
                         here = jnp.logical_and(y_lo == core, side * 4 + depth == z)
-                    cell = depth * 4 + corners[corner]
                     send(
-                        outgoing.at[q * 64 + lines[dx] * 16 + cell], dst, core * 4 + lines[dx], side * 16 + cell,
+                        outgoing.at[base + lines[dx] * 4 + corners[corner]], dst,
+                        core * 4 + lines[dx], (side * 4 + depth) * 4 + corners[corner],
                         ret_send.at[layer], ret_recv.at[2 * layer + colour_here], here,
                     )
 
@@ -253,9 +256,9 @@
             device_id=(row, sibling), device_id_type=MESH,
         )
         exchange.start()
-        quadrant(layer, 0, mine_r[...], back)
+        quadrant(layer, 0, mine_r, back)
         exchange.wait_recv()
-        quadrant(layer, 1, swap[...], back)
+        quadrant(layer, 1, swap, back)
         exchange.wait_send()
 
     def finish(layer):

time: 68.7 us -> 68.7 us (level)
  no operation moved by 1% of the time
where the time goes in v3:
time: 68.7 us; the launch traced here: 68.6 us
  Pallas kernels  67.9 us (99%)
  local copies, waits for them, and re-layouts  0.71 us (1%)
    pallas_call x1, Pallas kernels, shards(): pl.pallas_call(kernel, out_shape=pltpu.VMEM((TR, TC, CH), BF16), in_specs...  67.9 us

profile of v3, /device:TPU:1, one launch (start us, length us, event | category | flops | bytes accessed | tf_op | source)
XLA Modules:
  0.0 68.6 jit_solution(684754853443595837)
XLA Ops:
  0.0 67.9 %shard_map.91 = bf16[64,16,128]{2,1,0:T(8,128)(2,1)S(1)} custom-call(bf16[64,16,128]{2,1,0:T(8,128)(2,1)} %pair_hbm.1, s32[1,512]{1,0:T(1,128)} %bitcast.1, f32[2,128]{1,0:T(2,128)} %gain_hbm.1, f32[2,128]{1,0:T(2,128)} %bias_hbm.1, bf16[2,128,512]{2,1,0:T(8,128)(2,1)} %wp_hbm.1, bf16[2,128,128]{2,1,0:T(8,128)(2,1)} %wg_hbm.1, f32[2,128]{1,0:T(2,128)} %ogain_hbm.1, ...), custom_call_target="tpu_custom_call" | custom-call | flops 700000000 | bytes 4000000 | tf_op jit(solution)/shard_map/pallas_call | solution.py:330
  67.9 0.7 %copy.11 = bf16[64,16,128]{2,1,0:T(8,128)(2,1)} copy(bf16[64,16,128]{2,1,0:T(8,128)(2,1)S(1)} %shard_map.91) | data formatting | bytes 524288

commit v4 on v3

--- a/solution.py
+++ b/solution.py
@@ -19,8 +19,8 @@
     out_ref,
     pair_ref, mask_in, gain_ref, bias_ref, wp_ref, wg_ref, ogain_ref, obias_ref, wo_ref,
     wide, cur, gate, stage, masks, means, rstds, normed, wpt, wgt, wot, gains,
-    tile, recv1, recv2, back1, back2, swap1, swap2, mine_r, mine_l, mine_l2, raw_r, outgoing,
-    load_sem, hop_sem, send_sem, in_sem, swap_send, swap_recv, ret_send, ret_recv,
+    tile, recv1, recv2, back1, back2, swap1, swap2, mine_r, mine_l, mine_l2, raw_r, outgoing, relay,
+    load_sem, hop_sem, send_sem, in_sem, swap_send, swap_recv, ret_send, ret_recv, relay_sem, pass_send,
 ):
     row = lax.axis_index("row")
     col = lax.axis_index("col")
@@ -32,6 +32,8 @@
     colour_here = lax.rem(x + z, 2)
     own = (colour_here * 8 + z) * 8 + x // 2 * 4 + y_hi * 2 + y_lo
     z_low = lax.rem(z, 4)
+    relay_col = lax.rem(col + 24, 32)
+    served_z = lax.rem(z + 2, 8)
 
     loads = [
         pltpu.make_async_copy(src, dst, load_sem.at[n])
@@ -143,7 +145,8 @@
 
         @pl.loop(0, 8)
         def _(g):
-            colour, step = g // 4, lax.rem(g, 4)
+            colour = jnp.where(g == 0, 1, g // 5)
+            step = jnp.where(g == 0, 1, jnp.where(g < 5, g - 1, jnp.where(g == 5, 0, g - 4)))
             ahead = jnp.where(step == 0, 3, jnp.where(step == 1, 4, 4 - step))
             depths = [lax.rem(z + ahead, 8), lax.rem(z + jnp.where(step == 1, 0, 8 - ahead), 8)]
             blocks = [colour * 8 + depth for depth in depths]
@@ -164,12 +167,41 @@
                         for n in range(2):
                             here = None
                             if n == 1 and dx + dh + dl == 0:
-                                here = jnp.logical_and(g == 4 * colour_here + 1, to_core == core)
-                            send(
-                                tile.at[blocks[n] * 8 + halves[dx] * 4 + highs[dh] * 2 + lows[dl]], dst,
-                                lows[dl] * 4 + halves[dx] * 2 + odd[n], depths[n] * 4 + highs[dh] * 2 + to_core,
-                                send_sem.at[layer], in_sem.at[8 * layer + z], here,
-                            )
+                                here = jnp.logical_and(jnp.logical_and(step == 1, colour == colour_here), to_core == core)
+                            src = tile.at[blocks[n] * 8 + halves[dx] * 4 + highs[dh] * 2 + lows[dl]]
+
+                            def straight():
+                                send(
+                                    src, dst,
+                                    lows[dl] * 4 + halves[dx] * 2 + odd[n], depths[n] * 4 + highs[dh] * 2 + to_core,
+                                    send_sem.at[layer], in_sem.at[8 * layer + z], here,
+                                )
+
+                            def around():
+                                send(
+                                    src, relay.at[layer, dx * 4 + dh * 2 + dl], row, relay_col,
+                                    send_sem.at[layer], relay_sem.at[layer], None,
+                                )
+
+                            if n == 0:
+                                pl.when(g == 0)(around)
+                                pl.when(g > 0)(straight)
+                            else:
+                                straight()
+
+        held = relay.at[layer]
+        arrived(held, relay_sem.at[layer])
+        served_slot = served_z * 16 + x * 4 + corner if layer == 0 else lax.rem(served_z, 4) * 32 + row * 4 + corner
+        served_core = y_lo if layer == 0 else served_z // 4
+        beyond = lax.rem(z + 6, 8)
+        for dx in (1, 0):
+            for dh in (1, 0):
+                for dl in (1, 0):
+                    send(
+                        held.at[dx * 4 + dh * 2 + dl], (recv1 if layer == 0 else recv2).at[served_slot],
+                        lows[dl] * 4 + halves[dx] * 2 + lax.rem(1 + z, 2), beyond * 4 + highs[dh] * 2 + served_core,
+                        pass_send.at[layer], in_sem.at[8 * layer + served_z], None,
+                    )
 
         return to_core == core
 
@@ -192,7 +224,7 @@
         for step in range(8 if layer == 0 else 4):
             if layer == 0:
                 recv, width, pairs = recv1, 16, 2
-                place = lax.rem(z + (5, 3, 4, 0, 6, 2, 7, 1)[step], 8)
+                place = lax.rem(z + (5, 3, 0, 6, 2, 7, 1, 4)[step], 8)
                 sem = in_sem.at[place]
             else:
                 recv, width, pairs = recv2, 32, 4
@@ -320,6 +352,8 @@
             stage[pl.ds(256 * g + 16 * e + 2 * s + b, 8, stride=32), :] = values[8 * n : 8 * n + 8]
     out_ref[...] = stage[...].reshape(TR, TC, CH).astype(BF16)
     sent(outgoing, ret_send.at[1], home1)
+    for layer in range(2):
+        arrived(relay.at[layer], pass_send.at[layer])
 
 
 def shards(pair, residue_mask, in_gain, in_bias, proj_weight, gate_weight, out_gain, out_bias, out_weight):
@@ -357,9 +391,10 @@
             pltpu.VMEM((256, 512), BF16),
             pltpu.VMEM((512, 256), F32),
             pltpu.VMEM((CH, 8, CH), BF16),
+            pltpu.VMEM((2, 8, 16, CH), BF16),
             dma((9,)),
             pltpu.SemaphoreType.REGULAR,
-            dma((2,)), dma((16,)), dma((2,)), dma((2,)), dma((2,)), dma((4,)),
+            dma((2,)), dma((16,)), dma((2,)), dma((2,)), dma((2,)), dma((4,)), dma((2,)), dma((2,)),
         ],
         compiler_params=pltpu.CompilerParams(
             collective_id=0, has_side_effects=True, vmem_limit_bytes=48 * 1024 * 1024

time: 68.7 us -> 71.7 us (1.044)
  Pallas kernels: 67.9 us -> 70.9 us
    pallas_call x1, Pallas kernels: 67.9 us -> 70.9 us  [shards(): pl.pallas_call(kernel, out_shape=pltpu.VMEM((TR, TC, CH), BF16), in_specs...]
where the time goes in v4:
time: 71.7 us; the launch traced here: 71.6 us
  Pallas kernels  70.9 us (99%)
    pallas_call x1, Pallas kernels, shards(): pl.pallas_call(kernel, out_shape=pltpu.VMEM((TR, TC, CH), BF16), in_specs...  70.9 us

profile of v4, /device:TPU:1, one launch (start us, length us, event | category | flops | bytes accessed | tf_op | source)
XLA Modules:
  0.0 71.6 jit_solution(5825773354261297239)
XLA Ops:
  0.0 70.9 %shard_map.91 = bf16[64,16,128]{2,1,0:T(8,128)(2,1)S(1)} custom-call(bf16[64,16,128]{2,1,0:T(8,128)(2,1)} %pair_hbm.1, s32[1,512]{1,0:T(1,128)} %bitcast.1, f32[2,128]{1,0:T(2,128)} %gain_hbm.1, f32[2,128]{1,0:T(2,128)} %bias_hbm.1, bf16[2,128,512]{2,1,0:T(8,128)(2,1)} %wp_hbm.1, bf16[2,128,128]{2,1,0:T(8,128)(2,1)} %wg_hbm.1, f32[2,128]{1,0:T(2,128)} %ogain_hbm.1, ...), custom_call_target="tpu_custom_call" | custom-call | flops 700000000 | bytes 4000000 | tf_op jit(solution)/shard_map/pallas_call | solution.py:364
  70.9 0.7 copy.11

commit v5 on v3

--- a/solution.py
+++ b/solution.py
@@ -70,10 +70,10 @@
         even_b = jnp.sum(jnp.where(number == TC * col + 2 * sub, mask, 0.0), axis=1, keepdims=True)
         odd_b = jnp.sum(jnp.where(number == TC * col + 2 * sub + 1, mask, 0.0), axis=1, keepdims=True)
         mask_b = jnp.where(lane < 64, even_b, odd_b)
-        lane_n = lax.broadcasted_iota(jnp.int32, (512, CH), 1)
-        row_n = lax.broadcasted_iota(jnp.int32, (512, CH), 0)
-        a_of = ((lane_n // 16) % 4) * 16 + ((lane_n // 8) % 2) + 2 * (lane_n % 8)
-        pick = jnp.where(row_n == TR * row + a_of, 1.0, 0.0).astype(BF16)
+        place = lax.broadcasted_iota(jnp.int32, (1, CH), 1)
+        place = place - jnp.where(place >= 64, 64, 0)
+        a_of = 16 * (place // 16) + (place // 8) % 2 + 2 * (place % 8)
+        pick = jnp.where(lax.broadcasted_iota(jnp.int32, (512, CH), 0) == TR * row + a_of, 1.0, 0.0).astype(BF16)
         mask_a = jnp.dot(jnp.broadcast_to(mask, (8, 512)).astype(BF16), pick, preferred_element_type=F32)
         masks[...] = mask_a * mask_b
 
@@ -144,8 +144,7 @@
         @pl.loop(0, 8)
         def _(g):
             colour, step = g // 4, lax.rem(g, 4)
-            ahead = jnp.where(step == 0, 3, jnp.where(step == 1, 4, 4 - step))
-            depths = [lax.rem(z + ahead, 8), lax.rem(z + jnp.where(step == 1, 0, 8 - ahead), 8)]
+            depths = [lax.rem(z + 4 + step, 8), lax.rem(z + 3 - step, 8)]
             blocks = [colour * 8 + depth for depth in depths]
             weights = jnp.concatenate([wpt[layer, block] for block in blocks], axis=0)
             proj = jnp.dot(weights, normed[...], preferred_element_type=F32)
@@ -164,7 +163,7 @@
                         for n in range(2):
                             here = None
                             if n == 1 and dx + dh + dl == 0:
-                                here = jnp.logical_and(g == 4 * colour_here + 1, to_core == core)
+                                here = jnp.logical_and(g == 4 * colour_here + 3, to_core == core)
                             send(
                                 tile.at[blocks[n] * 8 + halves[dx] * 4 + highs[dh] * 2 + lows[dl]], dst,
                                 lows[dl] * 4 + halves[dx] * 2 + odd[n], depths[n] * 4 + highs[dh] * 2 + to_core,
@@ -192,7 +191,7 @@
         for step in range(8 if layer == 0 else 4):
             if layer == 0:
                 recv, width, pairs = recv1, 16, 2
-                place = lax.rem(z + (5, 3, 4, 0, 6, 2, 7, 1)[step], 8)
+                place = lax.rem(z + (4, 5, 3, 6, 2, 7, 1, 0)[step], 8)
                 sem = in_sem.at[place]
             else:
                 recv, width, pairs = recv2, 32, 4
@@ -288,11 +287,13 @@
         update = jnp.dot(wot[layer], out_normed.astype(BF16), preferred_element_type=F32)
         return cur[s] + gate[s] * update
 
-    for load in loads:
-        load.wait()
+    loads[1].wait()
+    make_masks()
+    for n in (2, 3, 4):
+        loads[n].wait()
     prepare(0)
-    make_masks()
     second_hop()
+    loads[0].wait()
     wide[...] = pair_ref[...].astype(F32).reshape(POS, CH)
     for s in range(8):
         rows = [wide[pl.ds(256 * g + 16 * e + 2 * s + b, 8, stride=32), :] for b, g, e in order]
@@ -300,6 +301,8 @@
     pl.semaphore_wait(hop_sem, COLS - 1)
     home1 = scatter(0)
     multiply(0)
+    for n in (5, 6, 7, 8):
+        loads[n].wait()
     prepare_out(0)
     make_gate(0)
     prepare(1)

time: 68.7 us -> 69 us (level)
  no operation moved by 1% of the time
where the time goes in v5:
time: 69 us; the launch traced here: 68.9 us
  Pallas kernels  68.2 us (99%)
  local copies, waits for them, and re-layouts  0.71 us (1%)
    pallas_call x1, Pallas kernels, shards(): pl.pallas_call(kernel, out_shape=pltpu.VMEM((TR, TC, CH), BF16), in_specs...  68.2 us

profile of v5, /device:TPU:1, one launch (start us, length us, event | category | flops | bytes accessed | tf_op | source)
XLA Modules:
  0.0 68.9 jit_solution(830610205952378673)
XLA Ops:
  0.0 68.2 %shard_map.91 = bf16[64,16,128]{2,1,0:T(8,128)(2,1)S(1)} custom-call(bf16[64,16,128]{2,1,0:T(8,128)(2,1)} %pair_hbm.1, s32[1,512]{1,0:T(1,128)} %bitcast.1, f32[2,128]{1,0:T(2,128)} %gain_hbm.1, f32[2,128]{1,0:T(2,128)} %bias_hbm.1, bf16[2,128,512]{2,1,0:T(8,128)(2,1)} %wp_hbm.1, bf16[2,128,128]{2,1,0:T(8,128)(2,1)} %wg_hbm.1, f32[2,128]{1,0:T(2,128)} %ogain_hbm.1, ...), custom_call_target="tpu_custom_call" | custom-call | flops 700000000 | bytes 4000000 | tf_op jit(solution)/shard_map/pallas_call | solution.py:333
  68.2 0.7 %copy.11 = bf16[64,16,128]{2,1,0:T(8,128)(2,1)} copy(bf16[64,16,128]{2,1,0:T(8,128)(2,1)S(1)} %shard_map.91) | data formatting | bytes 524288

commit v6 on v5

--- a/solution.py
+++ b/solution.py
@@ -29,8 +29,7 @@
     x, y_lo = lax.rem(row, 4), row // 4
     z, y_hi = col // 4, lax.rem(col // 2, 2)
 
-    colour_here = lax.rem(x + z, 2)
-    own = (colour_here * 8 + z) * 8 + x // 2 * 4 + y_hi * 2 + y_lo
+    own = (y_lo * 8 + z) * 8 + x * 2 + y_hi
     z_low = lax.rem(z, 4)
 
     loads = [
@@ -137,15 +136,14 @@
         corner = y_hi * 2 + core
         slot = z * 16 + x * 4 + corner if layer == 0 else z_low * 32 + row * 4 + corner
         dst = (recv1 if layer == 0 else recv2).at[slot]
-        lows = [y_lo, 1 - y_lo]
         highs = [y_hi, 1 - y_hi]
-        halves = [x // 2, 1 - x // 2]
+        columns = [lax.rem(x + d, 4) for d in range(4)]
 
         @pl.loop(0, 8)
         def _(g):
-            colour, step = g // 4, lax.rem(g, 4)
+            step, low = g // 2, lax.rem(y_lo + g, 2)
             depths = [lax.rem(z + 4 + step, 8), lax.rem(z + 3 - step, 8)]
-            blocks = [colour * 8 + depth for depth in depths]
+            blocks = [low * 8 + depth for depth in depths]
             weights = jnp.concatenate([wpt[layer, block] for block in blocks], axis=0)
             proj = jnp.dot(weights, normed[...], preferred_element_type=F32)
             left = jnp.concatenate([jax.nn.sigmoid(proj[n : n + 8]) * proj[n + 8 : n + 16] for n in (0, 32)], axis=0)
@@ -156,19 +154,17 @@
                 stage[pl.ds(s + 8, 16, stride=16), :] = right[:, CH * s : CH * s + CH] * keep
             for n, block in enumerate(blocks):
                 tile[pl.ds(block * 8, 8)] = stage[128 * n : 128 * n + 128, :].reshape(8, 16, CH).astype(BF16)
-            odd = [lax.rem(colour + depth, 2) for depth in depths]
-            for dx in (1, 0):
+            for dx in (2, 1, 3, 0):
                 for dh in (1, 0):
-                    for dl in (1, 0):
-                        for n in range(2):
-                            here = None
-                            if n == 1 and dx + dh + dl == 0:
-                                here = jnp.logical_and(g == 4 * colour_here + 3, to_core == core)
-                            send(
-                                tile.at[blocks[n] * 8 + halves[dx] * 4 + highs[dh] * 2 + lows[dl]], dst,
-                                lows[dl] * 4 + halves[dx] * 2 + odd[n], depths[n] * 4 + highs[dh] * 2 + to_core,
-                                send_sem.at[layer], in_sem.at[8 * layer + z], here,
-                            )
+                    for n in range(2):
+                        here = None
+                        if n == 1 and dx + dh == 0:
+                            here = jnp.logical_and(g == 6, to_core == core)
+                        send(
+                            tile.at[blocks[n] * 8 + columns[dx] * 2 + highs[dh]], dst,
+                            low * 4 + columns[dx], depths[n] * 4 + highs[dh] * 2 + to_core,
+                            send_sem.at[layer], in_sem.at[8 * layer + z], here,
+                        )
 
         return to_core == core
 
@@ -243,7 +239,7 @@
                     send(
                         outgoing.at[base + lines[dx] * 4 + corners[corner]], dst,
                         core * 4 + lines[dx], (side * 4 + depth) * 4 + corners[corner],
-                        ret_send.at[layer], ret_recv.at[2 * layer + colour_here], here,
+                        ret_send.at[layer], ret_recv.at[2 * layer + y_lo], here,
                     )
 
     def multiply(layer):
@@ -263,16 +259,16 @@
     def finish(layer):
         back = back1 if layer == 0 else back2
         halves = []
-        for colour in range(2):
-            arrived(back.at[pl.ds(64 * colour, 64)], ret_recv.at[2 * layer + colour])
+        for part_y in range(2):
+            arrived(back.at[pl.ds(64 * part_y, 64)], ret_recv.at[2 * layer + part_y])
             total = jnp.zeros((8, CH), F32)
-            for g in range(4 * colour, 4 * colour + 4):
+            for g in range(4 * part_y, 4 * part_y + 4):
                 part = back[16 * g : 16 * g + 16].astype(F32)
                 wide[128 * g : 128 * g + 128, :] = part.reshape(128, CH)
                 total = total + jnp.sum(part, axis=0)
             mean = total * (1.0 / 64)
             total = jnp.zeros((8, CH), F32)
-            for g in range(4 * colour, 4 * colour + 4):
+            for g in range(4 * part_y, 4 * part_y + 4):
                 part = wide[128 * g : 128 * g + 128, :].reshape(16, 8, CH) - mean[None]
                 total = total + jnp.sum(part * part, axis=0)
             halves.append((mean, total))

time: 69 us -> 70.9 us (1.028)
  Pallas kernels: 68.2 us -> 70.1 us
    pallas_call x1, Pallas kernels: 68.2 us -> 70.1 us  [shards(): pl.pallas_call(kernel, out_shape=pltpu.VMEM((TR, TC, CH), BF16), in_specs...]
where the time goes in v6:
time: 70.9 us; the launch traced here: 70.8 us
  Pallas kernels  70.1 us (99%)
  local copies, waits for them, and re-layouts  0.71 us (1%)
    pallas_call x1, Pallas kernels, shards(): pl.pallas_call(kernel, out_shape=pltpu.VMEM((TR, TC, CH), BF16), in_specs...  70.1 us

profile of v6, /device:TPU:1, one launch (start us, length us, event | category | flops | bytes accessed | tf_op | source)
XLA Modules:
  0.0 70.8 jit_solution(266112711701196017)
XLA Ops:
  0.0 70.1 %shard_map.91 = bf16[64,16,128]{2,1,0:T(8,128)(2,1)S(1)} custom-call(bf16[64,16,128]{2,1,0:T(8,128)(2,1)} %pair_hbm.1, s32[1,512]{1,0:T(1,128)} %bitcast.1, f32[2,128]{1,0:T(2,128)} %gain_hbm.1, f32[2,128]{1,0:T(2,128)} %bias_hbm.1, bf16[2,128,512]{2,1,0:T(8,128)(2,1)} %wp_hbm.1, bf16[2,128,128]{2,1,0:T(8,128)(2,1)} %wg_hbm.1, f32[2,128]{1,0:T(2,128)} %ogain_hbm.1, ...), custom_call_target="tpu_custom_call" | custom-call | flops 700000000 | bytes 4000000 | tf_op jit(solution)/shard_map/pallas_call | solution.py:329
  70.1 0.7 copy.11

commit v7 on v5

--- a/solution.py
+++ b/solution.py
@@ -29,9 +29,9 @@
     x, y_lo = lax.rem(row, 4), row // 4
     z, y_hi = col // 4, lax.rem(col // 2, 2)
 
-    colour_here = lax.rem(x + z, 2)
-    own = (colour_here * 8 + z) * 8 + x // 2 * 4 + y_hi * 2 + y_lo
     z_low = lax.rem(z, 4)
+    colour_here = lax.rem(x + 4 - z_low, 4)
+    own = (colour_here * 4 + z_low) * 8 + z // 4 * 4 + y_hi * 2 + y_lo
 
     loads = [
         pltpu.make_async_copy(src, dst, load_sem.at[n])
@@ -139,13 +139,13 @@
         dst = (recv1 if layer == 0 else recv2).at[slot]
         lows = [y_lo, 1 - y_lo]
         highs = [y_hi, 1 - y_hi]
-        halves = [x // 2, 1 - x // 2]
+        sides = [z // 4, 1 - z // 4]
 
         @pl.loop(0, 8)
         def _(g):
-            colour, step = g // 4, lax.rem(g, 4)
-            depths = [lax.rem(z + 4 + step, 8), lax.rem(z + 3 - step, 8)]
-            blocks = [colour * 8 + depth for depth in depths]
+            colour, step = g // 2, lax.rem(g, 2)
+            depths = [lax.rem(z_low + 3 - step, 4), lax.rem(z_low + step, 4)]
+            blocks = [colour * 4 + depth for depth in depths]
             weights = jnp.concatenate([wpt[layer, block] for block in blocks], axis=0)
             proj = jnp.dot(weights, normed[...], preferred_element_type=F32)
             left = jnp.concatenate([jax.nn.sigmoid(proj[n : n + 8]) * proj[n + 8 : n + 16] for n in (0, 32)], axis=0)
@@ -156,17 +156,17 @@
                 stage[pl.ds(s + 8, 16, stride=16), :] = right[:, CH * s : CH * s + CH] * keep
             for n, block in enumerate(blocks):
                 tile[pl.ds(block * 8, 8)] = stage[128 * n : 128 * n + 128, :].reshape(8, 16, CH).astype(BF16)
-            odd = [lax.rem(colour + depth, 2) for depth in depths]
-            for dx in (1, 0):
+            columns = [lax.rem(colour + depth, 4) for depth in depths]
+            for dz in (1, 0):
                 for dh in (1, 0):
                     for dl in (1, 0):
                         for n in range(2):
                             here = None
-                            if n == 1 and dx + dh + dl == 0:
-                                here = jnp.logical_and(g == 4 * colour_here + 3, to_core == core)
+                            if n == 1 and dz + dh + dl == 0:
+                                here = jnp.logical_and(g == 2 * colour_here, to_core == core)
                             send(
-                                tile.at[blocks[n] * 8 + halves[dx] * 4 + highs[dh] * 2 + lows[dl]], dst,
-                                lows[dl] * 4 + halves[dx] * 2 + odd[n], depths[n] * 4 + highs[dh] * 2 + to_core,
+                                tile.at[blocks[n] * 8 + sides[dz] * 4 + highs[dh] * 2 + lows[dl]], dst,
+                                lows[dl] * 4 + columns[n], (sides[dz] * 4 + depths[n]) * 4 + highs[dh] * 2 + to_core,
                                 send_sem.at[layer], in_sem.at[8 * layer + z], here,
                             )
 
@@ -191,11 +191,11 @@
         for step in range(8 if layer == 0 else 4):
             if layer == 0:
                 recv, width, pairs = recv1, 16, 2
-                place = lax.rem(z + (4, 5, 3, 6, 2, 7, 1, 0)[step], 8)
+                place = lax.rem(z + (5, 1, 4, 0, 6, 2, 7, 3)[step], 8)
                 sem = in_sem.at[place]
             else:
                 recv, width, pairs = recv2, 32, 4
-                place = far_first(step, z // 4 == core)
+                place = lax.rem(z_low + (1, 0, 2, 3)[step], 4)
                 sem = in_sem.at[8 + core * 4 + place]
             arrived(recv.at[pl.ds(place * width, width)], sem)
             rows = pl.ds(64 * step if layer == 0 else pl.multiple_of(place * 64, 64), 64)
@@ -243,7 +243,7 @@
                     send(
                         outgoing.at[base + lines[dx] * 4 + corners[corner]], dst,
                         core * 4 + lines[dx], (side * 4 + depth) * 4 + corners[corner],
-                        ret_send.at[layer], ret_recv.at[2 * layer + colour_here], here,
+                        ret_send.at[layer], ret_recv.at[2 * layer + colour_here // 2], here,
                     )
 
     def multiply(layer):

time: 69 us -> 68.8 us (level)
  no operation moved by 1% of the time
where the time goes in v7:
time: 68.8 us; the launch traced here: 68.7 us
  Pallas kernels  68 us (99%)
  local copies, waits for them, and re-layouts  0.71 us (1%)
    pallas_call x1, Pallas kernels, shards(): pl.pallas_call(kernel, out_shape=pltpu.VMEM((TR, TC, CH), BF16), in_specs...  68 us

profile of v7, /device:TPU:1, one launch (start us, length us, event | category | flops | bytes accessed | tf_op | source)
XLA Modules:
  0.0 68.7 jit_solution(6411074821464146045)
XLA Ops:
  0.0 68.0 %shard_map.91 = bf16[64,16,128]{2,1,0:T(8,128)(2,1)S(1)} custom-call(bf16[64,16,128]{2,1,0:T(8,128)(2,1)} %pair_hbm.1, s32[1,512]{1,0:T(1,128)} %bitcast.1, f32[2,128]{1,0:T(2,128)} %gain_hbm.1, f32[2,128]{1,0:T(2,128)} %bias_hbm.1, bf16[2,128,512]{2,1,0:T(8,128)(2,1)} %wp_hbm.1, bf16[2,128,128]{2,1,0:T(8,128)(2,1)} %wg_hbm.1, f32[2,128]{1,0:T(2,128)} %ogain_hbm.1, ...), custom_call_target="tpu_custom_call" | custom-call | flops 700000000 | bytes 4000000 | tf_op jit(solution)/shard_map/pallas_call | solution.py:333
  68.0 0.7 %copy.11 = bf16[64,16,128]{2,1,0:T(8,128)(2,1)} copy(bf16[64,16,128]{2,1,0:T(8,128)(2,1)S(1)} %shard_map.91) | data formatting | bytes 524288

commit v8 on v7

--- a/solution.py
+++ b/solution.py
@@ -98,7 +98,7 @@
         center = values - jnp.mean(values, axis=0, keepdims=True)
         spread = jnp.mean(center * center, axis=0, keepdims=True)
         scaled = center * lax.rsqrt(spread + 1e-05) * gains[layer, 0] + gains[layer, 1]
-        normed[:, CH * s : CH * s + CH] = scaled.astype(BF16)
+        normed[:, pl.ds(pl.multiple_of(s * CH, CH), CH)] = scaled.astype(BF16)
         cur[s] = values
 
     def send(src, dst, to_row, to_col, send_sem, recv_sem, here):
@@ -173,9 +173,10 @@
         return to_core == core
 
     def make_gate(layer):
-        for s in range(8):
-            part = jnp.dot(wgt[layer], normed[:, CH * s : CH * s + CH], preferred_element_type=F32)
-            gate[s] = jax.nn.sigmoid(part)
+        @pl.loop(0, 8)
+        def _(s):
+            part = normed[:, pl.ds(pl.multiple_of(s * CH, CH), CH)]
+            gate[s] = jax.nn.sigmoid(jnp.dot(wgt[layer], part, preferred_element_type=F32))
 
     def merge(first, second):
         low = lax.broadcasted_iota(jnp.int32, first.shape, 2) < 64
@@ -188,33 +189,34 @@
         return jnp.where(falling, 3 - step, step)
 
     def gather(layer):
-        for step in range(8 if layer == 0 else 4):
+        def collect(recv, width, place, p):
+            first = recv[pl.ds(place * width + 8 * p, 4)].astype(F32)
+            second = recv[pl.ds(place * width + 8 * p + 4, 4)].astype(F32)
+            even, odd = merge(first, second)
+            left = jnp.concatenate([even[:, :8], odd[:, :8]], axis=1).reshape(64, CH)
+            right = jnp.concatenate([even[:, 8:], odd[:, 8:]], axis=1).reshape(64, CH)
+            return left.astype(BF16), right
+
+        @pl.loop(0, 4)
+        def _(step):
+            low = lax.rem(z_low + jnp.where(step < 2, 1 - step, step), 4)
             if layer == 0:
-                recv, width, pairs = recv1, 16, 2
-                place = lax.rem(z + (5, 1, 4, 0, 6, 2, 7, 3)[step], 8)
-                sem = in_sem.at[place]
+                block = pl.ds(pl.multiple_of(step * 128, 128), 128)
+                for half in range(2):
+                    place = low + 4 * half
+                    arrived(recv1.at[pl.ds(place * 16, 16)], in_sem.at[place])
+                    rows = pl.ds(pl.multiple_of(step * 128 + 64 * half, 64), 64)
+                    for p in range(2):
+                        mine_l[rows, 128 * p : 128 * p + 128], raw_r[rows, 128 * p : 128 * p + 128] = collect(recv1, 16, place, p)
+                for p in range(2):
+                    mine_r[128 * p : 128 * p + 128, block] = raw_r[block, 128 * p : 128 * p + 128].T.astype(BF16)
             else:
-                recv, width, pairs = recv2, 32, 4
-                place = lax.rem(z_low + (1, 0, 2, 3)[step], 4)
-                sem = in_sem.at[8 + core * 4 + place]
-            arrived(recv.at[pl.ds(place * width, width)], sem)
-            rows = pl.ds(64 * step if layer == 0 else pl.multiple_of(place * 64, 64), 64)
-            for p in range(pairs):
-                first = recv[pl.ds(place * width + 8 * p, 4)].astype(F32)
-                second = recv[pl.ds(place * width + 8 * p + 4, 4)].astype(F32)
-                even, odd = merge(first, second)
-                left = jnp.concatenate([even[:, :8], odd[:, :8]], axis=1).reshape(64, CH)
-                right = jnp.concatenate([even[:, 8:], odd[:, 8:]], axis=1).reshape(64, CH)
-                lanes = slice(128 * p, 128 * p + 128)
-                if layer == 0:
-                    mine_l[rows, lanes] = left.astype(BF16)
-                    raw_r[rows, lanes] = right
-                else:
-                    mine_l2[rows, lanes] = left.astype(BF16)
-                    mine_r[rows, lanes] = right.astype(BF16)
-                if layer == 0 and step % 2 == 1:
-                    block = slice(64 * step - 64, 64 * step + 64)
-                    mine_r[lanes, block] = raw_r[block, lanes].T.astype(BF16)
+                arrived(recv2.at[pl.ds(low * 32, 32)], in_sem.at[8 + core * 4 + low])
+                rows = pl.ds(pl.multiple_of(low * 64, 64), 64)
+                for p in range(4):
+                    left, right = collect(recv2, 32, low, p)
+                    mine_l2[rows, 128 * p : 128 * p + 128] = left
+                    mine_r[rows, 128 * p : 128 * p + 128] = right.astype(BF16)
 
     def quadrant(layer, q, right, dst):
         side = core if q == 0 else 1 - core
@@ -263,19 +265,22 @@
     def finish(layer):
         back = back1 if layer == 0 else back2
         halves = []
-        for colour in range(2):
-            arrived(back.at[pl.ds(64 * colour, 64)], ret_recv.at[2 * layer + colour])
-            total = jnp.zeros((8, CH), F32)
-            for g in range(4 * colour, 4 * colour + 4):
-                part = back[16 * g : 16 * g + 16].astype(F32)
-                wide[128 * g : 128 * g + 128, :] = part.reshape(128, CH)
-                total = total + jnp.sum(part, axis=0)
-            mean = total * (1.0 / 64)
-            total = jnp.zeros((8, CH), F32)
-            for g in range(4 * colour, 4 * colour + 4):
-                part = wide[128 * g : 128 * g + 128, :].reshape(16, 8, CH) - mean[None]
-                total = total + jnp.sum(part * part, axis=0)
-            halves.append((mean, total))
+        zero = jnp.zeros((8, CH), F32)
+        for part in range(2):
+            arrived(back.at[pl.ds(64 * part, 64)], ret_recv.at[2 * layer + part])
+
+            def add(g, total):
+                values = back[pl.ds(64 * part + 16 * g, 16)].astype(F32)
+                wide[pl.ds(pl.multiple_of(512 * part + 128 * g, 128), 128), :] = values.reshape(128, CH)
+                return total + jnp.sum(values, axis=0)
+
+            mean = lax.fori_loop(0, 4, add, zero) * (1.0 / 64)
+
+            def vary(g, total):
+                values = wide[pl.ds(pl.multiple_of(512 * part + 128 * g, 128), 128), :].reshape(16, 8, CH) - mean[None]
+                return total + jnp.sum(values * values, axis=0)
+
+            halves.append((mean, lax.fori_loop(0, 4, vary, zero)))
         (mean0, total0), (mean1, total1) = halves
         apart = 0.5 * (mean0 - mean1)
         means[...] = 0.5 * (mean0 + mean1)
@@ -283,7 +288,7 @@
 
     def updated(layer, s):
         mixed = wide[pl.ds(s, CH, stride=8), :]
-        out_normed = (mixed - means[s : s + 1, :]) * rstds[s : s + 1, :] * gains[layer, 2] + gains[layer, 3]
+        out_normed = (mixed - means[pl.ds(s, 1), :]) * rstds[pl.ds(s, 1), :] * gains[layer, 2] + gains[layer, 3]
         update = jnp.dot(wot[layer], out_normed.astype(BF16), preferred_element_type=F32)
         return cur[s] + gate[s] * update
 
@@ -295,7 +300,8 @@
     second_hop()
     loads[0].wait()
     wide[...] = pair_ref[...].astype(F32).reshape(POS, CH)
-    for s in range(8):
+    @pl.loop(0, 8)
+    def _(s):
         rows = [wide[pl.ds(256 * g + 16 * e + 2 * s + b, 8, stride=32), :] for b, g, e in order]
         normalize(0, s, jnp.concatenate(rows, axis=0).T)
     pl.semaphore_wait(hop_sem, COLS - 1)
@@ -309,7 +315,8 @@
     prepare_out(1)
     sent(tile, send_sem.at[0], home1)
     finish(0)
-    for s in range(8):
+    @pl.loop(0, 8)
+    def _(s):
         normalize(1, s, updated(0, s).astype(BF16).astype(F32))
     home2 = scatter(1)
     sent(outgoing, ret_send.at[0], home1)
@@ -317,7 +324,8 @@
     make_gate(1)
     sent(tile, send_sem.at[1], home2)
     finish(1)
-    for s in range(8):
+    @pl.loop(0, 8)
+    def _(s):
         values = updated(1, s).T
         for n, (b, g, e) in enumerate(order):
             stage[pl.ds(256 * g + 16 * e + 2 * s + b, 8, stride=32), :] = values[8 * n : 8 * n + 8]

time: 68.8 us -> 72.1 us (1.048)
  Pallas kernels: 68 us -> 71.3 us
    pallas_call x1, Pallas kernels: 68 us -> 71.3 us  [shards(): pl.pallas_call(kernel, out_shape=pltpu.VMEM((TR, TC, CH), BF16), in_specs...]
where the time goes in v8:
time: 72.1 us; the launch traced here: 72 us
  Pallas kernels  71.3 us (99%)
    pallas_call x1, Pallas kernels, shards(): pl.pallas_call(kernel, out_shape=pltpu.VMEM((TR, TC, CH), BF16), in_specs...  71.3 us

profile of v8, /device:TPU:1, one launch (start us, length us, event | category | flops | bytes accessed | tf_op | source)
XLA Modules:
  0.0 72.0 jit_solution(10584934619175848642)
XLA Ops:
  0.0 71.3 %shard_map.91 = bf16[64,16,128]{2,1,0:T(8,128)(2,1)S(1)} custom-call(bf16[64,16,128]{2,1,0:T(8,128)(2,1)} %pair_hbm.1, s32[1,512]{1,0:T(1,128)} %bitcast.1, f32[2,128]{1,0:T(2,128)} %gain_hbm.1, f32[2,128]{1,0:T(2,128)} %bias_hbm.1, bf16[2,128,512]{2,1,0:T(8,128)(2,1)} %wp_hbm.1, bf16[2,128,128]{2,1,0:T(8,128)(2,1)} %wg_hbm.1, f32[2,128]{1,0:T(2,128)} %ogain_hbm.1, ...), custom_call_target="tpu_custom_call" | custom-call | flops 700000000 | bytes 4000000 | tf_op jit(solution)/shard_map/pallas_call | solution.py:341
  71.3 0.7 copy.11

commit v9 on v7

--- a/solution.py
+++ b/solution.py
@@ -94,12 +94,15 @@
         spread_out(ogain_ref, layer, 2)
         spread_out(obias_ref, layer, 3)
 
-    def normalize(layer, s, values):
+    def twice(value):
+        return jnp.concatenate([value, value], axis=1)
+
+    def normalize(layer, t, values):
         center = values - jnp.mean(values, axis=0, keepdims=True)
         spread = jnp.mean(center * center, axis=0, keepdims=True)
-        scaled = center * lax.rsqrt(spread + 1e-05) * gains[layer, 0] + gains[layer, 1]
-        normed[:, CH * s : CH * s + CH] = scaled.astype(BF16)
-        cur[s] = values
+        scaled = center * lax.rsqrt(spread + 1e-05) * twice(gains[layer, 0]) + twice(gains[layer, 1])
+        normed[:, 256 * t : 256 * t + 256] = scaled.astype(BF16)
+        cur[t] = values
 
     def send(src, dst, to_row, to_col, send_sem, recv_sem, here):
         def local():
@@ -173,9 +176,9 @@
         return to_core == core
 
     def make_gate(layer):
-        for s in range(8):
-            part = jnp.dot(wgt[layer], normed[:, CH * s : CH * s + CH], preferred_element_type=F32)
-            gate[s] = jax.nn.sigmoid(part)
+        for t in range(4):
+            part = jnp.dot(wgt[layer], normed[:, 256 * t : 256 * t + 256], preferred_element_type=F32)
+            gate[t] = jax.nn.sigmoid(part)
 
     def merge(first, second):
         low = lax.broadcasted_iota(jnp.int32, first.shape, 2) < 64
@@ -281,11 +284,14 @@
         means[...] = 0.5 * (mean0 + mean1)
         rstds[...] = lax.rsqrt((total0 + total1) * (1.0 / CH) + apart * apart + 1e-05)
 
-    def updated(layer, s):
-        mixed = wide[pl.ds(s, CH, stride=8), :]
-        out_normed = (mixed - means[s : s + 1, :]) * rstds[s : s + 1, :] * gains[layer, 2] + gains[layer, 3]
+    def updated(layer, t):
+        pair_of = [2 * t, 2 * t + 1]
+        mixed = jnp.concatenate([wide[pl.ds(s, CH, stride=8), :] for s in pair_of], axis=1)
+        mean = jnp.concatenate([means[s : s + 1, :] for s in pair_of], axis=1)
+        rstd = jnp.concatenate([rstds[s : s + 1, :] for s in pair_of], axis=1)
+        out_normed = (mixed - mean) * rstd * twice(gains[layer, 2]) + twice(gains[layer, 3])
         update = jnp.dot(wot[layer], out_normed.astype(BF16), preferred_element_type=F32)
-        return cur[s] + gate[s] * update
+        return cur[t] + gate[t] * update
 
     loads[1].wait()
     make_masks()
@@ -295,9 +301,11 @@
     second_hop()
     loads[0].wait()
     wide[...] = pair_ref[...].astype(F32).reshape(POS, CH)
-    for s in range(8):
-        rows = [wide[pl.ds(256 * g + 16 * e + 2 * s + b, 8, stride=32), :] for b, g, e in order]
-        normalize(0, s, jnp.concatenate(rows, axis=0).T)
+    for t in range(4):
+        rows = [
+            wide[pl.ds(256 * g + 16 * e + 2 * s + b, 8, stride=32), :] for s in (2 * t, 2 * t + 1) for b, g, e in order
+        ]
+        normalize(0, t, jnp.concatenate(rows, axis=0).T)
     pl.semaphore_wait(hop_sem, COLS - 1)
     home1 = scatter(0)
     multiply(0)
@@ -309,17 +317,17 @@
     prepare_out(1)
     sent(tile, send_sem.at[0], home1)
     finish(0)
-    for s in range(8):
-        normalize(1, s, updated(0, s).astype(BF16).astype(F32))
+    for t in range(4):
+        normalize(1, t, updated(0, t).astype(BF16).astype(F32))
     home2 = scatter(1)
     sent(outgoing, ret_send.at[0], home1)
     multiply(1)
     make_gate(1)
     sent(tile, send_sem.at[1], home2)
     finish(1)
-    for s in range(8):
-        values = updated(1, s).T
-        for n, (b, g, e) in enumerate(order):
+    for t in range(4):
+        values = updated(1, t).T
+        for n, (s, (b, g, e)) in enumerate([(s, place) for s in (2 * t, 2 * t + 1) for place in order]):
             stage[pl.ds(256 * g + 16 * e + 2 * s + b, 8, stride=32), :] = values[8 * n : 8 * n + 8]
     out_ref[...] = stage[...].reshape(TR, TC, CH).astype(BF16)
     sent(outgoing, ret_send.at[1], home1)
@@ -337,8 +345,8 @@
         out_specs=pl.BlockSpec(memory_space=pltpu.VMEM),
         scratch_shapes=[pltpu.VMEM(value.shape, value.dtype) for value in arguments] + [
             pltpu.VMEM((POS, CH), F32),
-            pltpu.VMEM((8, CH, CH), F32),
-            pltpu.VMEM((8, CH, CH), F32),
+            pltpu.VMEM((4, CH, 256), F32),
+            pltpu.VMEM((4, CH, 256), F32),
             pltpu.VMEM((POS, CH), F32),
             pltpu.VMEM((8, CH), F32),
             pltpu.VMEM((8, CH), F32),

time: 68.8 us -> 68.8 us (level)
  no operation moved by 1% of the time
where the time goes in v9:
time: 68.8 us; the launch traced here: 68.7 us
  Pallas kernels  68 us (99%)
  local copies, waits for them, and re-layouts  0.71 us (1%)
    pallas_call x1, Pallas kernels, shards(): pl.pallas_call(kernel, out_shape=pltpu.VMEM((TR, TC, CH), BF16), in_specs...  68 us

profile of v9, /device:TPU:1, one launch (start us, length us, event | category | flops | bytes accessed | tf_op | source)
XLA Modules:
  0.0 68.7 jit_solution(10622618093447812133)
XLA Ops:
  0.0 68.0 %shard_map.91 = bf16[64,16,128]{2,1,0:T(8,128)(2,1)S(1)} custom-call(bf16[64,16,128]{2,1,0:T(8,128)(2,1)} %pair_hbm.1, s32[1,512]{1,0:T(1,128)} %bitcast.1, f32[2,128]{1,0:T(2,128)} %gain_hbm.1, f32[2,128]{1,0:T(2,128)} %bias_hbm.1, bf16[2,128,512]{2,1,0:T(8,128)(2,1)} %wp_hbm.1, bf16[2,128,128]{2,1,0:T(8,128)(2,1)} %wg_hbm.1, f32[2,128]{1,0:T(2,128)} %ogain_hbm.1, ...), custom_call_target="tpu_custom_call" | custom-call | flops 700000000 | bytes 4000000 | tf_op jit(solution)/shard_map/pallas_call | solution.py:341
  68.0 0.7 %copy.11 = bf16[64,16,128]{2,1,0:T(8,128)(2,1)} copy(bf16[64,16,128]{2,1,0:T(8,128)(2,1)S(1)} %shard_map.91) | data formatting | bytes 524288

commit v10 on v9

--- a/solution.py
+++ b/solution.py
@@ -144,29 +144,29 @@
         highs = [y_hi, 1 - y_hi]
         sides = [z // 4, 1 - z // 4]
 
-        @pl.loop(0, 8)
-        def _(g):
-            colour, step = g // 2, lax.rem(g, 2)
-            depths = [lax.rem(z_low + 3 - step, 4), lax.rem(z_low + step, 4)]
+        @pl.loop(0, 4)
+        def _(colour):
+            depths = [lax.rem(z_low + d, 4) for d in (3, 0, 2, 1)]
             blocks = [colour * 4 + depth for depth in depths]
             weights = jnp.concatenate([wpt[layer, block] for block in blocks], axis=0)
             proj = jnp.dot(weights, normed[...], preferred_element_type=F32)
-            left = jnp.concatenate([jax.nn.sigmoid(proj[n : n + 8]) * proj[n + 8 : n + 16] for n in (0, 32)], axis=0)
-            right = jnp.concatenate([jax.nn.sigmoid(proj[n : n + 8]) * proj[n + 8 : n + 16] for n in (16, 48)], axis=0)
-            for s in range(8):
-                keep = masks[s : s + 1, :]
-                stage[pl.ds(s, 16, stride=16), :] = left[:, CH * s : CH * s + CH] * keep
-                stage[pl.ds(s + 8, 16, stride=16), :] = right[:, CH * s : CH * s + CH] * keep
             for n, block in enumerate(blocks):
+                part = proj[32 * n : 32 * n + 32]
+                left = jax.nn.sigmoid(part[0:8]) * part[8:16]
+                right = jax.nn.sigmoid(part[16:24]) * part[24:32]
+                for s in range(8):
+                    keep = masks[s : s + 1, :]
+                    stage[pl.ds(128 * n + s, 8, stride=16), :] = left[:, CH * s : CH * s + CH] * keep
+                    stage[pl.ds(128 * n + s + 8, 8, stride=16), :] = right[:, CH * s : CH * s + CH] * keep
                 tile[pl.ds(block * 8, 8)] = stage[128 * n : 128 * n + 128, :].reshape(8, 16, CH).astype(BF16)
             columns = [lax.rem(colour + depth, 4) for depth in depths]
-            for dz in (1, 0):
-                for dh in (1, 0):
-                    for dl in (1, 0):
-                        for n in range(2):
+            for n in range(4):
+                for dz in (1, 0):
+                    for dh in (1, 0):
+                        for dl in (1, 0):
                             here = None
                             if n == 1 and dz + dh + dl == 0:
-                                here = jnp.logical_and(g == 2 * colour_here, to_core == core)
+                                here = jnp.logical_and(colour == colour_here, to_core == core)
                             send(
                                 tile.at[blocks[n] * 8 + sides[dz] * 4 + highs[dh] * 2 + lows[dl]], dst,
                                 lows[dl] * 4 + columns[n], (sides[dz] * 4 + depths[n]) * 4 + highs[dh] * 2 + to_core,

time: 68.8 us -> 71.1 us (1.033)
  Pallas kernels: 68 us -> 70.3 us
    pallas_call x1, Pallas kernels: 68 us -> 70.3 us  [shards(): pl.pallas_call(kernel, out_shape=pltpu.VMEM((TR, TC, CH), BF16), in_specs...]
where the time goes in v10:
time: 71.1 us; the launch traced here: 71 us
  Pallas kernels  70.3 us (99%)
    pallas_call x1, Pallas kernels, shards(): pl.pallas_call(kernel, out_shape=pltpu.VMEM((TR, TC, CH), BF16), in_specs...  70.3 us

profile of v10, /device:TPU:1, one launch (start us, length us, event | category | flops | bytes accessed | tf_op | source)
XLA Modules:
  0.0 71.0 jit_solution(16776491440380678011)
XLA Ops:
  0.0 70.3 %shard_map.91 = bf16[64,16,128]{2,1,0:T(8,128)(2,1)S(1)} custom-call(bf16[64,16,128]{2,1,0:T(8,128)(2,1)} %pair_hbm.1, s32[1,512]{1,0:T(1,128)} %bitcast.1, f32[2,128]{1,0:T(2,128)} %gain_hbm.1, f32[2,128]{1,0:T(2,128)} %bias_hbm.1, bf16[2,128,512]{2,1,0:T(8,128)(2,1)} %wp_hbm.1, bf16[2,128,128]{2,1,0:T(8,128)(2,1)} %wg_hbm.1, f32[2,128]{1,0:T(2,128)} %ogain_hbm.1, ...), custom_call_target="tpu_custom_call" | custom-call | flops 700000000 | bytes 4000000 | tf_op jit(solution)/shard_map/pallas_call | solution.py:341
  70.3 0.7 copy.11

commit v11 on v9

--- a/solution.py
+++ b/solution.py
@@ -14,11 +14,15 @@
 POS = TR * TC
 
 
+def sigmoid(values):
+    return 0.5 * jnp.tanh(0.5 * values) + 0.5
+
+
 def kernel(
     pair_hbm, mask_hbm, gain_hbm, bias_hbm, wp_hbm, wg_hbm, ogain_hbm, obias_hbm, wo_hbm,
     out_ref,
     pair_ref, mask_in, gain_ref, bias_ref, wp_ref, wg_ref, ogain_ref, obias_ref, wo_ref,
-    wide, cur, gate, stage, masks, means, rstds, normed, wpt, wgt, wot, gains,
+    wide, cur, gate, stage, masks, means, rstds, normed, wpt, proj_all, wgt, wot, gains,
     tile, recv1, recv2, back1, back2, swap1, swap2, mine_r, mine_l, mine_l2, raw_r, outgoing,
     load_sem, hop_sem, send_sem, in_sem, swap_send, swap_recv, ret_send, ret_recv,
 ):
@@ -84,7 +88,7 @@
         turned = wp_ref[layer].astype(F32).T
         for b in range(16):
             rows = [turned[128 * q + 8 * b : 128 * q + 8 * b + 8] for q in range(4)]
-            wpt[layer, b] = jnp.concatenate(rows, axis=0).astype(BF16)
+            wpt[layer, 32 * b : 32 * b + 32] = jnp.concatenate(rows, axis=0).astype(BF16)
         spread_out(gain_ref, layer, 0)
         spread_out(bias_ref, layer, 1)
 
@@ -101,7 +105,9 @@
         center = values - jnp.mean(values, axis=0, keepdims=True)
         spread = jnp.mean(center * center, axis=0, keepdims=True)
         scaled = center * lax.rsqrt(spread + 1e-05) * twice(gains[layer, 0]) + twice(gains[layer, 1])
-        normed[:, 256 * t : 256 * t + 256] = scaled.astype(BF16)
+        part = scaled.astype(BF16)
+        normed[:, 256 * t : 256 * t + 256] = part
+        proj_all[:, 256 * t : 256 * t + 256] = jnp.dot(wpt[layer], part, preferred_element_type=F32)
         cur[t] = values
 
     def send(src, dst, to_row, to_col, send_sem, recv_sem, here):
@@ -149,15 +155,12 @@
             colour, step = g // 2, lax.rem(g, 2)
             depths = [lax.rem(z_low + 3 - step, 4), lax.rem(z_low + step, 4)]
             blocks = [colour * 4 + depth for depth in depths]
-            weights = jnp.concatenate([wpt[layer, block] for block in blocks], axis=0)
-            proj = jnp.dot(weights, normed[...], preferred_element_type=F32)
-            left = jnp.concatenate([jax.nn.sigmoid(proj[n : n + 8]) * proj[n + 8 : n + 16] for n in (0, 32)], axis=0)
-            right = jnp.concatenate([jax.nn.sigmoid(proj[n : n + 8]) * proj[n + 8 : n + 16] for n in (16, 48)], axis=0)
-            for s in range(8):
-                keep = masks[s : s + 1, :]
-                stage[pl.ds(s, 16, stride=16), :] = left[:, CH * s : CH * s + CH] * keep
-                stage[pl.ds(s + 8, 16, stride=16), :] = right[:, CH * s : CH * s + CH] * keep
             for n, block in enumerate(blocks):
+                for s in range(8):
+                    part = proj_all[pl.ds(pl.multiple_of(block * 32, 32), 32), CH * s : CH * s + CH]
+                    keep = masks[s : s + 1, :]
+                    stage[pl.ds(128 * n + s, 8, stride=16), :] = sigmoid(part[0:8]) * part[8:16] * keep
+                    stage[pl.ds(128 * n + s + 8, 8, stride=16), :] = sigmoid(part[16:24]) * part[24:32] * keep
                 tile[pl.ds(block * 8, 8)] = stage[128 * n : 128 * n + 128, :].reshape(8, 16, CH).astype(BF16)
             columns = [lax.rem(colour + depth, 4) for depth in depths]
             for dz in (1, 0):
@@ -178,7 +181,7 @@
     def make_gate(layer):
         for t in range(4):
             part = jnp.dot(wgt[layer], normed[:, 256 * t : 256 * t + 256], preferred_element_type=F32)
-            gate[t] = jax.nn.sigmoid(part)
+            gate[t] = sigmoid(part)
 
     def merge(first, second):
         low = lax.broadcasted_iota(jnp.int32, first.shape, 2) < 64
@@ -352,7 +355,8 @@
             pltpu.VMEM((8, CH), F32),
             pltpu.VMEM((8, CH), F32),
             pltpu.VMEM((CH, POS), BF16),
-            pltpu.VMEM((2, 16, 32, CH), BF16),
+            pltpu.VMEM((2, 512, CH), BF16),
+            pltpu.VMEM((512, POS), F32),
             pltpu.VMEM((2, CH, CH), BF16),
             pltpu.VMEM((2, CH, CH), BF16),
             pltpu.VMEM((2, 4, CH, CH), F32),

time: 68.8 us -> 69 us (level)
  no operation moved by 1% of the time
where the time goes in v11:
time: 69 us; the launch traced here: 68.9 us
  Pallas kernels  68.2 us (99%)
  local copies, waits for them, and re-layouts  0.71 us (1%)
    pallas_call x1, Pallas kernels, shards(): pl.pallas_call(kernel, out_shape=pltpu.VMEM((TR, TC, CH), BF16), in_specs...  68.2 us

profile of v11, /device:TPU:1, one launch (start us, length us, event | category | flops | bytes accessed | tf_op | source)
XLA Modules:
  0.0 68.9 jit_solution(4362670386878066312)
XLA Ops:
  0.0 68.2 %shard_map.91 = bf16[64,16,128]{2,1,0:T(8,128)(2,1)S(1)} custom-call(bf16[64,16,128]{2,1,0:T(8,128)(2,1)} %pair_hbm.1, s32[1,512]{1,0:T(1,128)} %bitcast.1, f32[2,128]{1,0:T(2,128)} %gain_hbm.1, f32[2,128]{1,0:T(2,128)} %bias_hbm.1, bf16[2,128,512]{2,1,0:T(8,128)(2,1)} %wp_hbm.1, bf16[2,128,128]{2,1,0:T(8,128)(2,1)} %wg_hbm.1, f32[2,128]{1,0:T(2,128)} %ogain_hbm.1, ...), custom_call_target="tpu_custom_call" | custom-call | flops 700000000 | bytes 4000000 | tf_op jit(solution)/shard_map/pallas_call | solution.py:344
  68.2 0.7 %copy.11 = bf16[64,16,128]{2,1,0:T(8,128)(2,1)} copy(bf16[64,16,128]{2,1,0:T(8,128)(2,1)S(1)} %shard_map.91) | data formatting | bytes 524288

commit v12 on v11

--- a/solution.py
+++ b/solution.py
@@ -163,18 +163,17 @@
                     stage[pl.ds(128 * n + s + 8, 8, stride=16), :] = sigmoid(part[16:24]) * part[24:32] * keep
                 tile[pl.ds(block * 8, 8)] = stage[128 * n : 128 * n + 128, :].reshape(8, 16, CH).astype(BF16)
             columns = [lax.rem(colour + depth, 4) for depth in depths]
-            for dz in (1, 0):
-                for dh in (1, 0):
-                    for dl in (1, 0):
-                        for n in range(2):
-                            here = None
-                            if n == 1 and dz + dh + dl == 0:
-                                here = jnp.logical_and(g == 2 * colour_here, to_core == core)
-                            send(
-                                tile.at[blocks[n] * 8 + sides[dz] * 4 + highs[dh] * 2 + lows[dl]], dst,
-                                lows[dl] * 4 + columns[n], (sides[dz] * 4 + depths[n]) * 4 + highs[dh] * 2 + to_core,
-                                send_sem.at[layer], in_sem.at[8 * layer + z], here,
-                            )
+            for m in range(16):
+                dz, n = 1 - m % 2, m // 2 % 2
+                dl, dh = 1 - m // 4 % 2, 1 - m // 8
+                here = None
+                if n == 1 and dz + dh + dl == 0:
+                    here = jnp.logical_and(g == 2 * colour_here, to_core == core)
+                send(
+                    tile.at[blocks[n] * 8 + sides[dz] * 4 + highs[dh] * 2 + lows[dl]], dst,
+                    lows[dl] * 4 + columns[n], (sides[dz] * 4 + depths[n]) * 4 + highs[dh] * 2 + to_core,
+                    send_sem.at[layer], in_sem.at[8 * layer + z], here,
+                )
 
         return to_core == core
 
@@ -188,10 +187,6 @@
         even = jnp.where(low, first, pltpu.roll(second, 64, 2))
         odd = jnp.where(low, pltpu.roll(first, 64, 2), second)
         return even, odd
-
-    def far_first(step, same):
-        falling = (z_low < 2) == same
-        return jnp.where(falling, 3 - step, step)
 
     def gather(layer):
         for step in range(8 if layer == 0 else 4):
@@ -225,32 +220,34 @@
     def quadrant(layer, q, right, dst):
         side = core if q == 0 else 1 - core
         lines = [lax.rem(x + n, 4) for n in range(4)]
-        corners = [(y_hi if dy == 0 else 1 - y_hi) * 2 + (core if dc == 0 else 1 - core) for dy in range(2) for dc in range(2)]
+        floors = [lax.rem(z_low + n, 4) for n in range(4)]
 
         @pl.loop(0, 4)
         def _(step):
-            depth = far_first(step, z // 4 == side)
-            rows = right[pl.ds(pl.multiple_of(depth * 64, 64), 64), :]
+            corner = lax.rem(y_hi + 1 - step // 2, 2) * 2 + lax.rem(core + 1 - lax.rem(step, 2), 2)
+            rows = jnp.concatenate(
+                [right[pl.ds(pl.multiple_of(64 * n + 16 * corner, 16), 16), :] for n in range(4)], axis=0
+            )
             if layer == 0:
                 mixed = jnp.dot(rows, mine_l[...], preferred_element_type=F32)
             else:
                 mixed = lax.dot_general(rows, mine_l2[...], (((1,), (1,)), ((), ())), preferred_element_type=F32)
-            base = q * 64 + depth * 16
+            base = q * 64 + corner * 16
             for p in range(2):
                 block = mixed[:, 128 * p : 128 * p + 128].reshape(4, 16, CH)
                 even, odd = merge(block[:, :8], block[:, 8:])
                 outgoing[pl.ds(base + 8 * p, 4)] = even.astype(BF16)
                 outgoing[pl.ds(base + 8 * p + 4, 4)] = odd.astype(BF16)
-            for corner in (3, 2, 1, 0):
-                for dx in (2, 1, 3, 0):
-                    here = None
-                    if corner == 0 and dx == 0:
-                        here = jnp.logical_and(y_lo == core, side * 4 + depth == z)
-                    send(
-                        outgoing.at[base + lines[dx] * 4 + corners[corner]], dst,
-                        core * 4 + lines[dx], (side * 4 + depth) * 4 + corners[corner],
-                        ret_send.at[layer], ret_recv.at[2 * layer + colour_here // 2], here,
-                    )
+            for n in range(16):
+                dx, dz = (2, 1, 3, 0)[(n + n // 4) % 4], (2, 1, 3, 0)[n % 4]
+                here = None
+                if dx == 0 and dz == 0:
+                    here = jnp.logical_and(step == 3, jnp.logical_and(y_lo == core, side == z // 4))
+                send(
+                    outgoing.at[base + lines[dx] * 4 + floors[dz]], dst,
+                    core * 4 + lines[dx], (side * 4 + floors[dz]) * 4 + corner,
+                    ret_send.at[layer], ret_recv.at[2 * layer + colour_here // 2], here,
+                )
 
     def multiply(layer):
         back = (back1 if layer == 0 else back2).at[own]

time: 69 us -> 70.4 us (1.020)
  Pallas kernels: 68.2 us -> 69.6 us
    pallas_call x1, Pallas kernels: 68.2 us -> 69.6 us  [shards(): pl.pallas_call(kernel, out_shape=pltpu.VMEM((TR, TC, CH), BF16), in_specs...]
where the time goes in v12:
time: 70.4 us; the launch traced here: 70.3 us
  Pallas kernels  69.6 us (99%)
  local copies, waits for them, and re-layouts  0.71 us (1%)
    pallas_call x1, Pallas kernels, shards(): pl.pallas_call(kernel, out_shape=pltpu.VMEM((TR, TC, CH), BF16), in_specs...  69.6 us

profile of v12, /device:TPU:1, one launch (start us, length us, event | category | flops | bytes accessed | tf_op | source)
XLA Modules:
  0.0 70.3 jit_solution(13374197589297867750)
XLA Ops:
  0.0 69.6 %shard_map.91 = bf16[64,16,128]{2,1,0:T(8,128)(2,1)S(1)} custom-call(bf16[64,16,128]{2,1,0:T(8,128)(2,1)} %pair_hbm.1, s32[1,512]{1,0:T(1,128)} %bitcast.1, f32[2,128]{1,0:T(2,128)} %gain_hbm.1, f32[2,128]{1,0:T(2,128)} %bias_hbm.1, bf16[2,128,512]{2,1,0:T(8,128)(2,1)} %wp_hbm.1, bf16[2,128,128]{2,1,0:T(8,128)(2,1)} %wg_hbm.1, f32[2,128]{1,0:T(2,128)} %ogain_hbm.1, ...), custom_call_target="tpu_custom_call" | custom-call | flops 700000000 | bytes 4000000 | tf_op jit(solution)/shard_map/pallas_call | solution.py:341
  69.6 0.7 %copy.11 = bf16[64,16,128]{2,1,0:T(8,128)(2,1)} copy(bf16[64,16,128]{2,1,0:T(8,128)(2,1)S(1)} %shard_map.91) | data formatting | bytes 524288

commit v13 on v11

--- a/solution.py
+++ b/solution.py
@@ -148,33 +148,41 @@
         dst = (recv1 if layer == 0 else recv2).at[slot]
         lows = [y_lo, 1 - y_lo]
         highs = [y_hi, 1 - y_hi]
-        sides = [z // 4, 1 - z // 4]
-
-        @pl.loop(0, 8)
-        def _(g):
-            colour, step = g // 2, lax.rem(g, 2)
-            depths = [lax.rem(z_low + 3 - step, 4), lax.rem(z_low + step, 4)]
-            blocks = [colour * 4 + depth for depth in depths]
-            for n, block in enumerate(blocks):
+
+        @pl.loop(0, 4)
+        def _(colour):
+            blocks = [colour * 4 + lax.rem(z_low + a, 4) for a in range(4)]
+            columns = [lax.rem(colour + z_low + a, 4) for a in range(4)]
+
+            def pack(a):
                 for s in range(8):
-                    part = proj_all[pl.ds(pl.multiple_of(block * 32, 32), 32), CH * s : CH * s + CH]
+                    part = proj_all[pl.ds(pl.multiple_of(blocks[a] * 32, 32), 32), CH * s : CH * s + CH]
                     keep = masks[s : s + 1, :]
-                    stage[pl.ds(128 * n + s, 8, stride=16), :] = sigmoid(part[0:8]) * part[8:16] * keep
-                    stage[pl.ds(128 * n + s + 8, 8, stride=16), :] = sigmoid(part[16:24]) * part[24:32] * keep
-                tile[pl.ds(block * 8, 8)] = stage[128 * n : 128 * n + 128, :].reshape(8, 16, CH).astype(BF16)
-            columns = [lax.rem(colour + depth, 4) for depth in depths]
-            for dz in (1, 0):
+                    stage[pl.ds(128 * a + s, 8, stride=16), :] = sigmoid(part[0:8]) * part[8:16] * keep
+                    stage[pl.ds(128 * a + s + 8, 8, stride=16), :] = sigmoid(part[16:24]) * part[24:32] * keep
+                tile[pl.ds(blocks[a] * 8, 8)] = stage[128 * a : 128 * a + 128, :].reshape(8, 16, CH).astype(BF16)
+
+            def deliver(shifts):
                 for dh in (1, 0):
                     for dl in (1, 0):
-                        for n in range(2):
+                        for shift in shifts:
+                            a, depth = shift % 4, lax.rem(z + shift, 8)
                             here = None
-                            if n == 1 and dz + dh + dl == 0:
-                                here = jnp.logical_and(g == 2 * colour_here, to_core == core)
+                            if shift + dh + dl == 0:
+                                here = jnp.logical_and(colour == colour_here, to_core == core)
                             send(
-                                tile.at[blocks[n] * 8 + sides[dz] * 4 + highs[dh] * 2 + lows[dl]], dst,
-                                lows[dl] * 4 + columns[n], (sides[dz] * 4 + depths[n]) * 4 + highs[dh] * 2 + to_core,
+                                tile.at[blocks[a] * 8 + depth // 4 * 4 + highs[dh] * 2 + lows[dl]], dst,
+                                lows[dl] * 4 + columns[a], depth * 4 + highs[dh] * 2 + to_core,
                                 send_sem.at[layer], in_sem.at[8 * layer + z], here,
                             )
+
+            pack(0)
+            pack(3)
+            deliver((4, 3))
+            pack(1)
+            pack(2)
+            deliver((5, 2, 6))
+            deliver((1, 7, 0))
 
         return to_core == core
 
@@ -197,7 +205,7 @@
         for step in range(8 if layer == 0 else 4):
             if layer == 0:
                 recv, width, pairs = recv1, 16, 2
-                place = lax.rem(z + (5, 1, 4, 0, 6, 2, 7, 3)[step], 8)
+                place = lax.rem(z + (4, 5, 3, 6, 2, 7, 1, 0)[step], 8)
                 sem = in_sem.at[place]
             else:
                 recv, width, pairs = recv2, 32, 4

time: 69 us -> 70.5 us (1.022)
  Pallas kernels: 68.2 us -> 69.7 us
    pallas_call x1, Pallas kernels: 68.2 us -> 69.7 us  [shards(): pl.pallas_call(kernel, out_shape=pltpu.VMEM((TR, TC, CH), BF16), in_specs...]
where the time goes in v13:
time: 70.5 us; the launch traced here: 70.4 us
  Pallas kernels  69.7 us (99%)
  local copies, waits for them, and re-layouts  0.71 us (1%)
    pallas_call x1, Pallas kernels, shards(): pl.pallas_call(kernel, out_shape=pltpu.VMEM((TR, TC, CH), BF16), in_specs...  69.7 us

profile of v13, /device:TPU:1, one launch (start us, length us, event | category | flops | bytes accessed | tf_op | source)
XLA Modules:
  0.0 70.4 jit_solution(1643321367112420308)
XLA Ops:
  0.0 69.7 %shard_map.91 = bf16[64,16,128]{2,1,0:T(8,128)(2,1)S(1)} custom-call(bf16[64,16,128]{2,1,0:T(8,128)(2,1)} %pair_hbm.1, s32[1,512]{1,0:T(1,128)} %bitcast.1, f32[2,128]{1,0:T(2,128)} %gain_hbm.1, f32[2,128]{1,0:T(2,128)} %bias_hbm.1, bf16[2,128,512]{2,1,0:T(8,128)(2,1)} %wp_hbm.1, bf16[2,128,128]{2,1,0:T(8,128)(2,1)} %wg_hbm.1, f32[2,128]{1,0:T(2,128)} %ogain_hbm.1, ...), custom_call_target="tpu_custom_call" | custom-call | flops 700000000 | bytes 4000000 | tf_op jit(solution)/shard_map/pallas_call | solution.py:352
  69.7 0.7 %copy.11 = bf16[64,16,128]{2,1,0:T(8,128)(2,1)} copy(bf16[64,16,128]{2,1,0:T(8,128)(2,1)S(1)} %shard_map.91) | data formatting | bytes 524288

commit v14 on v11

--- a/solution.py
+++ b/solution.py
@@ -162,6 +162,11 @@
                     stage[pl.ds(128 * n + s, 8, stride=16), :] = sigmoid(part[0:8]) * part[8:16] * keep
                     stage[pl.ds(128 * n + s + 8, 8, stride=16), :] = sigmoid(part[16:24]) * part[24:32] * keep
                 tile[pl.ds(block * 8, 8)] = stage[128 * n : 128 * n + 128, :].reshape(8, 16, CH).astype(BF16)
+            if layer == 0:
+                @pl.when(g == 0)
+                def _():
+                    pl.semaphore_wait(hop_sem, COLS - 1)
+
             columns = [lax.rem(colour + depth, 4) for depth in depths]
             for dz in (1, 0):
                 for dh in (1, 0):
@@ -301,7 +306,6 @@
     for n in (2, 3, 4):
         loads[n].wait()
     prepare(0)
-    second_hop()
     loads[0].wait()
     wide[...] = pair_ref[...].astype(F32).reshape(POS, CH)
     for t in range(4):
@@ -309,7 +313,8 @@
             wide[pl.ds(256 * g + 16 * e + 2 * s + b, 8, stride=32), :] for s in (2 * t, 2 * t + 1) for b, g, e in order
         ]
         normalize(0, t, jnp.concatenate(rows, axis=0).T)
-    pl.semaphore_wait(hop_sem, COLS - 1)
+        if t == 0:
+            second_hop()
     home1 = scatter(0)
     multiply(0)
     for n in (5, 6, 7, 8):

time: 69 us -> 68.9 us (level)
  no operation moved by 1% of the time
where the time goes in v14:
time: 68.9 us; the launch traced here: 68.8 us
  Pallas kernels  68.1 us (99%)
  local copies, waits for them, and re-layouts  0.71 us (1%)
    pallas_call x1, Pallas kernels, shards(): pl.pallas_call(kernel, out_shape=pltpu.VMEM((TR, TC, CH), BF16), in_specs...  68.1 us

profile of v14, /device:TPU:1, one launch (start us, length us, event | category | flops | bytes accessed | tf_op | source)
XLA Modules:
  0.0 68.8 jit_solution(477584290247418977)
XLA Ops:
  0.0 68.1 %shard_map.91 = bf16[64,16,128]{2,1,0:T(8,128)(2,1)S(1)} custom-call(bf16[64,16,128]{2,1,0:T(8,128)(2,1)} %pair_hbm.1, s32[1,512]{1,0:T(1,128)} %bitcast.1, f32[2,128]{1,0:T(2,128)} %gain_hbm.1, f32[2,128]{1,0:T(2,128)} %bias_hbm.1, bf16[2,128,512]{2,1,0:T(8,128)(2,1)} %wp_hbm.1, bf16[2,128,128]{2,1,0:T(8,128)(2,1)} %wg_hbm.1, f32[2,128]{1,0:T(2,128)} %ogain_hbm.1, ...), custom_call_target="tpu_custom_call" | custom-call | flops 700000000 | bytes 4000000 | tf_op jit(solution)/shard_map/pallas_call | solution.py:349
  68.1 0.7 %copy.11 = bf16[64,16,128]{2,1,0:T(8,128)(2,1)} copy(bf16[64,16,128]{2,1,0:T(8,128)(2,1)S(1)} %shard_map.91) | data formatting | bytes 524288

commit v15 on v14

--- a/solution.py
+++ b/solution.py
@@ -33,9 +33,9 @@
     x, y_lo = lax.rem(row, 4), row // 4
     z, y_hi = col // 4, lax.rem(col // 2, 2)
 
+    colour_here = lax.rem(x + z, 2)
+    own = (colour_here * 8 + z) * 8 + x // 2 * 4 + y_hi * 2 + y_lo
     z_low = lax.rem(z, 4)
-    colour_here = lax.rem(x + 4 - z_low, 4)
-    own = (colour_here * 4 + z_low) * 8 + z // 4 * 4 + y_hi * 2 + y_lo
 
     loads = [
         pltpu.make_async_copy(src, dst, load_sem.at[n])
@@ -148,13 +148,13 @@
         dst = (recv1 if layer == 0 else recv2).at[slot]
         lows = [y_lo, 1 - y_lo]
         highs = [y_hi, 1 - y_hi]
-        sides = [z // 4, 1 - z // 4]
+        halves = [x // 2, 1 - x // 2]
 
         @pl.loop(0, 8)
         def _(g):
-            colour, step = g // 2, lax.rem(g, 2)
-            depths = [lax.rem(z_low + 3 - step, 4), lax.rem(z_low + step, 4)]
-            blocks = [colour * 4 + depth for depth in depths]
+            colour, step = g // 4, lax.rem(g, 4)
+            depths = [lax.rem(z + 4 + step, 8), lax.rem(z + 3 - step, 8)]
+            blocks = [colour * 8 + depth for depth in depths]
             for n, block in enumerate(blocks):
                 for s in range(8):
                     part = proj_all[pl.ds(pl.multiple_of(block * 32, 32), 32), CH * s : CH * s + CH]
@@ -167,17 +167,17 @@
                 def _():
                     pl.semaphore_wait(hop_sem, COLS - 1)
 
-            columns = [lax.rem(colour + depth, 4) for depth in depths]
-            for dz in (1, 0):
+            odd = [lax.rem(colour + depth, 2) for depth in depths]
+            for dx in (1, 0):
                 for dh in (1, 0):
                     for dl in (1, 0):
                         for n in range(2):
                             here = None
-                            if n == 1 and dz + dh + dl == 0:
-                                here = jnp.logical_and(g == 2 * colour_here, to_core == core)
+                            if n == 1 and dx + dh + dl == 0:
+                                here = jnp.logical_and(g == 4 * colour_here + 3, to_core == core)
                             send(
-                                tile.at[blocks[n] * 8 + sides[dz] * 4 + highs[dh] * 2 + lows[dl]], dst,
-                                lows[dl] * 4 + columns[n], (sides[dz] * 4 + depths[n]) * 4 + highs[dh] * 2 + to_core,
+                                tile.at[blocks[n] * 8 + halves[dx] * 4 + highs[dh] * 2 + lows[dl]], dst,
+                                lows[dl] * 4 + halves[dx] * 2 + odd[n], depths[n] * 4 + highs[dh] * 2 + to_core,
                                 send_sem.at[layer], in_sem.at[8 * layer + z], here,
                             )
 
@@ -202,11 +202,11 @@
         for step in range(8 if layer == 0 else 4):
             if layer == 0:
                 recv, width, pairs = recv1, 16, 2
-                place = lax.rem(z + (5, 1, 4, 0, 6, 2, 7, 3)[step], 8)
+                place = lax.rem(z + (4, 5, 3, 6, 2, 7, 1, 0)[step], 8)
                 sem = in_sem.at[place]
             else:
                 recv, width, pairs = recv2, 32, 4
-                place = lax.rem(z_low + (1, 0, 2, 3)[step], 4)
+                place = far_first(step, z // 4 == core)
                 sem = in_sem.at[8 + core * 4 + place]
             arrived(recv.at[pl.ds(place * width, width)], sem)
             rows = pl.ds(64 * step if layer == 0 else pl.multiple_of(place * 64, 64), 64)
@@ -254,7 +254,7 @@
                     send(
                         outgoing.at[base + lines[dx] * 4 + corners[corner]], dst,
                         core * 4 + lines[dx], (side * 4 + depth) * 4 + corners[corner],
-                        ret_send.at[layer], ret_recv.at[2 * layer + colour_here // 2], here,
+                        ret_send.at[layer], ret_recv.at[2 * layer + colour_here], here,
                     )
 
     def multiply(layer):

time: 68.9 us -> 69.4 us (level)
  no operation moved by 1% of the time
where the time goes in v15:
time: 69.4 us; the launch traced here: 69.3 us
  Pallas kernels  68.6 us (99%)
  local copies, waits for them, and re-layouts  0.71 us (1%)
    pallas_call x1, Pallas kernels, shards(): pl.pallas_call(kernel, out_shape=pltpu.VMEM((TR, TC, CH), BF16), in_specs...  68.6 us

profile of v15, /device:TPU:1, one launch (start us, length us, event | category | flops | bytes accessed | tf_op | source)
XLA Modules:
  0.0 69.3 jit_solution(12603243676758863874)
XLA Ops:
  0.0 68.6 %shard_map.91 = bf16[64,16,128]{2,1,0:T(8,128)(2,1)S(1)} custom-call(bf16[64,16,128]{2,1,0:T(8,128)(2,1)} %pair_hbm.1, s32[1,512]{1,0:T(1,128)} %bitcast.1, f32[2,128]{1,0:T(2,128)} %gain_hbm.1, f32[2,128]{1,0:T(2,128)} %bias_hbm.1, bf16[2,128,512]{2,1,0:T(8,128)(2,1)} %wp_hbm.1, bf16[2,128,128]{2,1,0:T(8,128)(2,1)} %wg_hbm.1, f32[2,128]{1,0:T(2,128)} %ogain_hbm.1, ...), custom_call_target="tpu_custom_call" | custom-call | flops 700000000 | bytes 4000000 | tf_op jit(solution)/shard_map/pallas_call | solution.py:349
  68.6 0.7 %copy.11 = bf16[64,16,128]{2,1,0:T(8,128)(2,1)} copy(bf16[64,16,128]{2,1,0:T(8,128)(2,1)S(1)} %shard_map.91) | data formatting | bytes 524288
